TPU v7x, 128 devices: a whole 4x4x4 slice. The times are simulated.
128 devices in a mesh: dp: 8 (over z, core), rank: 16 (over x, y).
Axes of the slice: x: 4, y: 4, z: 4, core: 2. Of those that a mesh axis runs over, the one named last changes fastest.
Arguments:
- acts: bfloat16 [384, 256, 4096], P('dp', None, 'rank'), may hold values from -6 to 6
- grads: bfloat16 [384, 256, 11008], P('dp', None, 'rank'), may hold values from -6 to 6
- proj_in: bfloat16 [4096, 64], P('rank'), may hold values from -0.09375 to 0.09375
- proj_out: bfloat16 [11008, 64], P('rank'), may hold values from -0.0546875 to 0.0546875
- queries: float32 [4096, 4096], P('rank'), may hold values from -0.09375 to 0.09375
- seg_emb: int32 [384], P('dp'), may hold values from 0 to 15
- query_emb: int32 [4096], P('rank'), may hold values from 0 to 15
- compat: int32 [16, 16], replicated, may hold values from 0 to 1, as said below
- counts: int32 [384], P('dp'), may hold values from 32 to 256
Outputs:
- influence: float32 [384, 4096], P('dp', 'rank')
Inputs may be any that keep to these rules, and one draw needn't show every extreme that they name: compat has ones on its diagonal.
All inputs are finite; a program needn't handle non-finite values.
Results may differ from a plain program's by a relative error of at most 0.0003.
Values sent between devices are 32-bit elements; how exact they have to be, the bound alone decides.
No kernel may reach another device: no remote copies, remote signals or barrier semaphores. Data moves between devices by JAX's collectives and lax.ppermute only.
A program may use at most 128 MiB of HBM per device.

v0:
```python
import functools

import jax
import jax.numpy as jnp
import numpy as np
from jax import lax
from jax.experimental import pallas as pl
from jax.experimental.pallas import tpu as pltpu
from jax.sharding import PartitionSpec as P

SIDE = 4
RANKS = SIDE * SIDE
SLOTS = 3
BF16 = jnp.bfloat16
F32 = jnp.float32
LADDER = (544, 768)


def at(x, y):
    return (x % SIDE) * SIDE + y % SIDE


def home_x(rank):
    return sum(divmod(rank, SIDE)) % 2 == 0


def neighbour(home, flip, rank):
    x, y = divmod(rank, SIDE)
    return at(x ^ flip, y) if home == home_x(rank) else at(x, y ^ flip)


def stream_owner(home, stream, flip, rank):
    x, y = divmod(rank, SIDE)
    along_x = home == home_x(rank)
    via = neighbour(home, flip, rank)
    if along_x == home_x(via):
        return via if stream == 1 else second(3, via)
    return second(stream, via)


def second(kind, rank):
    x, y = divmod(rank, SIDE)
    even = (x + y) % 2 == 0
    if kind == 3:
        return at(x, y + 2) if even else at(x + 2, y)
    step = 1 if kind == 1 else -1
    return at(x + step, y) if even else at(x, y + step)


def destinations(rank):
    order = []
    for home, stream, flip in BLOCKS:
        order.append(stream_owner(home, stream, flip, rank))
    return order


BLOCKS = (
    [(True, 1, 1), (True, 1, 2), (False, 1, 1), (False, 1, 2)]
    + [(True, 2, 3), (True, 2, 2), (False, 2, 3), (False, 2, 2)]
    + [(True, 1, 3), (True, 2, 1), (False, 1, 3), (False, 2, 1)]
    + [(True, 1, 0), (True, 2, 0), (False, 1, 0), (False, 2, 0)]
)


def slot_positions(rank):
    zig = 7 - rank // 2 if rank % 2 == 0 else 15 - rank // 2
    sums = [r + (7 - r // 2 if r % 2 == 0 else 15 - r // 2) for r in range(RANKS)]
    above = sum(s > sums[rank] or (s == sums[rank] and r > rank) for r, s in enumerate(sums))
    return [rank, RANKS + zig, 2 * RANKS + above]


def gathered(rank):
    x, y = divmod(rank, SIDE)
    return [at(x - dx, y - dy) for dy in range(SIDE) for dx in range(SIDE)]


PROJECT_POS = np.array([sum((slot_positions(q) for q in destinations(r)), []) for r in range(RANKS)], np.int32)
GATHER_POS = np.array([sum((slot_positions(q) for q in gathered(r)), []) for r in range(RANKS)], np.int32)
OWNER_POS = np.array([slot_positions(q) for q in range(RANKS)], np.int32).T.reshape(-1)
FLIPS = {
    (home, flip): [(r, neighbour(home, flip, r)) for r in range(RANKS)] for home in (True, False) for flip in (1, 3)
}
SECOND = {kind: [(r, second(kind, r)) for r in range(RANKS)] for kind in (1, 2, 3)}


def shift(dx, dy):
    return [(r, at(r // SIDE + dx, r % SIDE + dy)) for r in range(RANKS)]


def up(n, m):
    return (n + (m - 1)) // m * m


def project_kernel(first, segs, cnts, acts, grads, w_in, w_out, *refs):
    outs, (act_buf, grad_buf, spill, sems) = refs[:4], refs[4:]
    toks = act_buf.shape[1]
    cap = outs[0].shape[0] // 2

    def copies(j):
        s = segs[first + j]
        return (
            pltpu.make_async_copy(acts.at[s], act_buf.at[j], sems.at[j, 0]),
            pltpu.make_async_copy(grads.at[s], grad_buf.at[j], sems.at[j, 1]),
        )

    for j in range(act_buf.shape[0]):
        for copy in copies(j):
            copy.start()
    w_a = jnp.concatenate([jnp.zeros_like(w_in[...]), w_in[...]], axis=0)
    nt = (((1,), (1,)), ((), ()))

    def rows(j):
        side_g = jnp.dot(w_out[...], grad_buf[j], preferred_element_type=F32)
        side_a = lax.dot_general(act_buf[j], w_a, nt, preferred_element_type=F32)
        return side_a + jnp.concatenate([side_g, jnp.zeros_like(side_g)], axis=0).T

    for h, out in enumerate(outs):

        def block(i, _):
            j = (h * 2 + i) * SLOTS
            for k in range(SLOTS):
                for copy in copies(j + k):
                    copy.wait()
            made = [rows(j + k) for k in range(SLOTS)]
            base = pl.multiple_of(i * cap, 8)
            mid = pl.multiple_of(base + up(cnts[first + j], 8), 8)
            last = pl.multiple_of(mid + up(cnts[first + j + 1], 8), 8)
            out[pl.ds(base, toks), :] = made[0]
            out[pl.ds(mid, toks), :] = made[1]
            spill[...] = made[2]

            def piece(n, _):
                to = pl.multiple_of(last + n * 16, 8)
                out[pl.ds(to, 16), :] = spill[pl.ds(pl.multiple_of(n * 16, 16), 16), :]
                return 0

            return lax.fori_loop(0, up(cnts[first + j + 2], 16) // 16, piece, 0)

        lax.fori_loop(0, 2, block, 0)


def project(part, cap, segs, cnts, acts, grads_t, w_in, w_out):
    toks, fa = acts.shape[1:]
    fg = grads_t.shape[1]
    n = acts.shape[0] // 2
    vmem = pl.BlockSpec(memory_space=pltpu.VMEM)
    smem = pl.BlockSpec(memory_space=pltpu.SMEM)
    any_ = pl.BlockSpec(memory_space=pl.ANY)
    return pl.pallas_call(
        functools.partial(project_kernel, part * n),
        in_specs=[smem, smem, any_, any_, vmem, vmem],
        out_specs=[vmem] * 4,
        out_shape=[jax.ShapeDtypeStruct((2 * cap, 128), F32)] * 4,
        scratch_shapes=[
            pltpu.VMEM((n, toks, fa), BF16),
            pltpu.VMEM((n, fg, toks), BF16),
            pltpu.VMEM((toks, 128), F32),
            pltpu.SemaphoreType.DMA((n, 2)),
        ],
        compiler_params=pltpu.CompilerParams(vmem_limit_bytes=56 * 2**20),
        cost_estimate=pl.CostEstimate(
            flops=n * toks * 2 * 64 * (fa + fg),
            bytes_accessed=n * toks * 2 * (fa + fg) + 8 * cap * 512,
            transcendentals=0,
        ),
        name="project",
    )(segs, cnts, acts, grads_t, w_in, w_out)


def split(x):
    hi = x.astype(BF16)
    return hi, (x - hi.astype(F32)).astype(BF16)


def outer_kernel(cnts, own, r1, r2, r3, out, pair):
    total = (own[...] + r1[...]) + (r2[...] + r3[...])
    cap = total.shape[0]
    row = lax.broadcasted_iota(jnp.int32, (cap, 128), 0)
    off1 = up(cnts[0], 8)
    off2 = off1 + up(cnts[1], 8)
    live = [
        row < cnts[0],
        (row >= off1) & (row < off1 + cnts[1]),
        (row >= off2) & (row < off2 + cnts[2]),
    ]
    total = jnp.where(live[0] | live[1] | live[2], total, 0.0)
    lane = lax.broadcasted_iota(jnp.int32, (cap, 128), 1)
    act = jnp.where(lane < 64, pltpu.roll(total, 64, 1), total)
    a_hi, a_lo = split(act)
    total_t = total.T[:64]
    col = lax.broadcasted_iota(jnp.int32, (64, cap), 1)
    live_t = [
        col < cnts[0],
        (col >= off1) & (col < off1 + cnts[1]),
        (col >= off2) & (col < off2 + cnts[2]),
    ]
    grad = jnp.concatenate([jnp.where(m, total_t, 0.0) for m in live_t], axis=0)
    g_hi, g_lo = split(grad)
    dot = functools.partial(jnp.dot, preferred_element_type=F32)
    pair[...] = dot(g_hi, a_hi) + (dot(g_hi, a_lo) + dot(g_lo, a_hi))
    first = pair[pl.ds(0, 96, stride=2), :]
    other = pair[pl.ds(1, 96, stride=2), :]
    lane = lax.broadcasted_iota(jnp.int32, (96, 128), 1)
    out[...] = jnp.where(lane < 64, first, other)


def outer(cnts, parts):
    cap = parts[0].shape[0]
    spec = pl.BlockSpec(memory_space=pltpu.VMEM)
    return pl.pallas_call(
        outer_kernel,
        in_specs=[pl.BlockSpec(memory_space=pltpu.SMEM)] + [spec] * 4,
        out_specs=spec,
        out_shape=jax.ShapeDtypeStruct((SLOTS * 32, 128), F32),
        scratch_shapes=[pltpu.VMEM((SLOTS * 64, 128), F32)],
        compiler_params=pltpu.CompilerParams(vmem_limit_bytes=24 * 2**20),
        cost_estimate=pl.CostEstimate(flops=6 * 192 * cap * 128, bytes_accessed=4 * cap * 512, transcendentals=0),
        name="outer",
    )(cnts, *parts)


def hop(x, pairs):
    return lax.ppermute(x, "rank", pairs)


def features(cap, segs, cnts, acts, grads_t, w_in, w_out):
    made = [project(part, cap, segs, cnts, acts, grads_t, w_in, w_out) for part in range(2)]
    made = [made[0][:2], made[0][2:], made[1][:2], made[1][2:]]
    flip = {1: 1, 2: 3}
    orders = [(stream, home) for stream in (1, 2) for home in (True, False)]
    got, onward, done = {}, {}, {}
    for stream, home in orders:
        got[not home, stream] = hop(made[stream - 1][0 if home else 1], FLIPS[home, flip[stream]])
    came = {}
    for stream, home in orders:
        at_b = made[2][0 if home else 1][(stream - 1) * cap : stream * cap]
        onward[home, stream] = at_b + got[home, stream][cap:]
        came[not home, stream] = hop(onward[home, stream], FLIPS[home, flip[3 - stream]])
    came[True, 1], came[False, 1], _, _ = lax.optimization_barrier(
        (came[True, 1], came[False, 1], onward[True, 2], onward[False, 2])
    )
    for stream, home in orders:
        stay = made[3][0 if home else 1][(stream - 1) * cap : stream * cap]
        done[home, stream] = (stay + got[home, stream][:cap]) + came[home, stream]
    parts = [
        done[True, 1],
        hop(done[False, 1], SECOND[1]),
        hop(done[False, 2], SECOND[2]),
        hop(done[True, 2], SECOND[3]),
    ]
    return outer(cnts[-4 * SLOTS :][:SLOTS], parts)


def halves_kernel(queries, hi, lo):
    hi[...], lo[...] = split(queries[...])


def halves(queries):
    nq, nf = queries.shape
    steps = 4
    spec = pl.BlockSpec((nq // steps, nf), lambda i: (i, 0))
    out = jax.ShapeDtypeStruct((nq, nf), BF16)
    return pl.pallas_call(
        halves_kernel,
        grid=(steps,),
        in_specs=[spec],
        out_specs=[spec, spec],
        out_shape=[out, out],
        compiler_params=pltpu.CompilerParams(vmem_limit_bytes=48 * 2**20),
        cost_estimate=pl.CostEstimate(flops=nq * nf * 2, bytes_accessed=nq * nf * 8, transcendentals=0),
        name="halves",
    )(queries)


def score_kernel(segs, *refs):
    feats, (q_hi, q_lo, seg_kind, query_kind, compat, raw_out, sums_out, placed) = refs[:4], refs[4:]
    n = placed.shape[0]
    nt = (((1,), (1,)), ((), ()))
    dot = functools.partial(lax.dot_general, dimension_numbers=nt, preferred_element_type=F32)
    width = q_hi.shape[1] // 128
    total = jnp.zeros(placed.shape, F32)
    for m in range(0, width, 2):
        left = jnp.concatenate(
            [
                jnp.concatenate([f[pl.ds(m + e, f.shape[0] // width, stride=width), :] for f in feats], axis=0)
                for e in range(2)
            ],
            axis=1,
        )
        l_hi, l_lo = split(left)
        cols = slice(m * 128, (m + 2) * 128)
        both = dot(jnp.concatenate([l_hi, l_lo], axis=0), q_hi[:, cols])
        total = total + ((both[:n] + both[n:]) + dot(l_hi, q_lo[:, cols]))
    placed[...] = total
    for slot in range(n):
        raw_out[pl.ds(segs[slot], 1), :] = placed[slot : slot + 1, :]
    kinds = compat.shape[0]
    one_seg = (seg_kind[...] == lax.broadcasted_iota(jnp.int32, (n, kinds), 1)).astype(F32)
    nq = query_kind.shape[1]
    one_query = (query_kind[...] == lax.broadcasted_iota(jnp.int32, (kinds, nq), 0)).astype(F32)
    table = jnp.dot(one_seg, compat[...].astype(F32), preferred_element_type=F32)
    allowed = jnp.dot(table, one_query, preferred_element_type=F32)
    raw = raw_out[...] * allowed
    raw_out[...] = raw
    sums_out[...] = jnp.broadcast_to(jnp.sum(raw * raw, axis=0, keepdims=True), sums_out.shape)


def score(segs, feats, q_hi, q_lo, seg_emb, query_emb, compat):
    n, (nq, nf) = segs.shape[0], q_hi.shape
    vmem = pl.BlockSpec(memory_space=pltpu.VMEM)
    return pl.pallas_call(
        score_kernel,
        in_specs=[pl.BlockSpec(memory_space=pltpu.SMEM)] + [vmem] * 9,
        out_specs=[vmem, vmem],
        out_shape=(jax.ShapeDtypeStruct((n, nq), F32), jax.ShapeDtypeStruct((8, nq), F32)),
        scratch_shapes=[pltpu.VMEM((n, nq), F32)],
        compiler_params=pltpu.CompilerParams(vmem_limit_bytes=24 * 2**20),
        cost_estimate=pl.CostEstimate(flops=6 * n * nq * nf, bytes_accessed=nq * nf * 4, transcendentals=0),
        name="score",
    )(segs, *feats, q_hi, q_lo, seg_emb[:, None], query_emb[None, :], compat)


def per_device(acts, grads, proj_in, proj_out, queries, seg_emb, query_emb, compat, counts):
    segs_here = acts.shape[0]
    me = lax.axis_index("rank")
    grads_t = jnp.swapaxes(grads, 1, 2)
    w_in, w_out = proj_in.T, proj_out.T

    ids = lax.iota(jnp.int32, segs_here)
    before = (counts[None, :] > counts[:, None]) | (
        (counts[None, :] == counts[:, None]) & (ids[None, :] < ids[:, None])
    )
    place = jnp.sum(before.astype(jnp.int32), axis=1)

    def pick(positions, values):
        return jnp.sum(jnp.where(positions[:, None] == place[None, :], values[None, :], 0), axis=1)

    mine = jnp.asarray(PROJECT_POS)[me]
    segs, cnts = pick(mine, ids), pick(mine, counts)
    segs_gathered = pick(jnp.asarray(GATHER_POS)[me], ids)

    held = pick(jnp.asarray(OWNER_POS), counts).reshape(SLOTS, RANKS)
    need = jnp.max(up(held[0], 8) + up(held[1], 8) + up(held[2], 16))
    rung = jnp.sum((need > jnp.asarray(LADDER[:-1])).astype(jnp.int32))
    branches = [functools.partial(features, cap) for cap in LADDER]
    owned = lax.switch(rung, branches, segs, cnts, acts, grads_t, w_in, w_out)
    queries, owned = lax.optimization_barrier((queries, owned))
    q_hi, q_lo = halves(queries)
    line = jnp.concatenate([owned] + [hop(owned, shift(d, 0)) for d in (1, 2, 3)], axis=0)
    feats = [line] + [hop(line, shift(0, d)) for d in (1, 2, 3)]
    groups = lax.axis_size("dp")
    raw, sums = score(segs_gathered, feats, q_hi, q_lo, seg_emb, query_emb, compat)

    total = sums
    for core, z in ((1, 0), (0, 1), (0, 3)):
        other = [(i, (i // 2 ^ z) * 2 + (i % 2 ^ core)) for i in range(groups)]
        total = total + lax.ppermute(total, "dp", other)
    power = total[:1] / (segs_here * groups)
    return raw / jnp.sqrt(power + 1e-06)


def solution(mesh):
    return jax.shard_map(
        per_device,
        mesh=mesh,
        in_specs=(
            P("dp", None, "rank"),
            P("dp", None, "rank"),
            P("rank", None),
            P("rank", None),
            P("rank", None),
            P("dp"),
            P("rank"),
            P(),
            P("dp"),
        ),
        out_specs=P("dp", "rank"),
        check_vma=False,
    )
```

profile of v0, /device:TPU:0, one launch (start us, length us, event | category | flops | bytes accessed | tf_op | source)
XLA Modules:
  0.0 92.2 jit_solution(10809610096734794753)
XLA Ops:
  3.9 55.4 %conditional.1 = (f32[96,128]{1,0:T(8,128)S(1)}) conditional(s32[]{:T(128)} %clamp.8, (s32[48]{0:T(128)S(1)}, s32[48]{0:T(128)S(1)}, bf16[48,256,256]{2,1,0:T(8,128)(2,1)}, bf16[48,688,256]{2,1,0:T(8,128)(2,1)}, bf16[64,256]{1,0:T(8,128)(2,1)}, /*index=5*/bf16[64,688]{1,0:T(8,128)(2,1)}) %tuple.34, (s32[48]{0:T(128)S(1)}, s32[48]{0:T(128)S(1)}, ...), branch_computations={%region_6.7_spmd, %region_7.8_spmd} | conditional | flops 1599209472 | bytes 91316864 | solution.py:346
  4.0 9.2 %project.5 = (f32[1088,128]{1,0:T(8,128)}, f32[1088,128]{1,0:T(8,128)}, f32[1088,128]{1,0:T(8,128)}, f32[1088,128]{1,0:T(8,128)}) custom-call(s32[48]{0:T(128)S(1)} %get-tuple-element.33.segs, s32[48]{0:T(128)S(1)} %get-tuple-element.32.cnts, bf16[48,256,256]{2,1,0:T(8,128)(2,1)} %get-tuple-element.34.acts, bf16[48,688,256]{2,1,0:T(8,128)(2,1)} %get-tuple-element.35.grads, ...), custom_call_target="tpu_custom_call" | custom-call | flops 742391808 | bytes 13828096 | tf_op jit(solution)/shard_map/cond/branch_0_fun/project/pallas_call | solution.py:149
  13.1 1.7 %collective-permute-start = (f32[1088,128]{1,0:T(8,128)}, f32[1088,128]{1,0:T(8,128)S(1)}, u32[]{:S(2)}, u32[]{:S(2)}) collective-permute-start(f32[1088,128]{1,0:T(8,128)} %get-tuple-element.39), channel_id=1, source_target_pairs={{0,1},{1,5},{2,3},{3,7},{4,0},{5,4},{6,2},{7,6},{8,9},{9,13},{10,1... | collective-permute-start | bytes 1671176 | tf_op jit(solution)/shard_map/cond/branch_0_fun/ppermute | solution.py:223
  14.9 3.4 %collective-permute-start.4 = (f32[1088,128]{1,0:T(8,128)}, f32[1088,128]{1,0:T(8,128)S(1)}, u32[]{:S(2)}, u32[]{:S(2)}) collective-permute-start(f32[1088,128]{1,0:T(8,128)} %get-tuple-element.43), channel_id=1, source_target_pairs={{0,3},{1,13},{2,1},{3,15},{4,8},{5,6},{6,10},{7,4},{8,11},{9,5},{1... | collective-permute-start | bytes 1671176 | tf_op jit(solution)/shard_map/cond/branch_0_fun/ppermute | solution.py:223
  18.2 1.8 %collective-permute-start.5 = (f32[1088,128]{1,0:T(8,128)}, f32[1088,128]{1,0:T(8,128)}, u32[]{:S(2)}, u32[]{:S(2)}) collective-permute-start(f32[1088,128]{1,0:T(8,128)} %get-tuple-element.44), channel_id=1, source_target_pairs={{0,12},{1,2},{2,14},{3,0},{4,7},{5,9},{6,5},{7,11},{8,4},{9,10},{1... | collective-permute-start | bytes 1671176 | tf_op jit(solution)/shard_map/cond/branch_0_fun/ppermute | solution.py:223
  20.0 10.9 %project.4 = (f32[1088,128]{1,0:T(8,128)}, f32[1088,128]{1,0:T(8,128)}, f32[1088,128]{1,0:T(8,128)}, f32[1088,128]{1,0:T(8,128)}) custom-call(s32[48]{0:T(128)S(1)} %get-tuple-element.33.segs, s32[48]{0:T(128)S(1)} %get-tuple-element.32.cnts, bf16[48,256,256]{2,1,0:T(8,128)(2,1)S(1)} %bitcast.14, bf16[48,688,256]{2,1,0:T(8,128)(2,1)} %get-tuple-element.35.grads, ...), custom_call_target="tpu_custom_call" | custom-call | flops 742391808 | bytes 13828096 | tf_op jit(solution)/shard_map/cond/branch_0_fun/project/pallas_call | solution.py:149
  34.9 1.9 %collective-permute-start.2 = (f32[544,128]{1,0:T(8,128)S(1)}, f32[544,128]{1,0:T(8,128)S(1)}, u32[]{:S(2)}, u32[]{:S(2)}) collective-permute-start(f32[544,128]{1,0:T(8,128)S(1)} %get-tuple-element.85), channel_id=1, source_target_pairs={{0,3},{1,13},{2,1},{3,15},{4,8},{5,6},{6,10},{7,4},{8,11},{9,5},{1... | collective-permute-start | bytes 835592 | tf_op jit(solution)/shard_map/cond/branch_0_fun/ppermute | solution.py:223
  38.8 2.0 %collective-permute-done.3 = f32[544,128]{1,0:T(8,128)S(1)} collective-permute-done((f32[544,128]{1,0:T(8,128)S(1)}, f32[544,128]{1,0:T(8,128)S(1)}, u32[]{:S(2)}, u32[]{:S(2)}) %collective-permute-start.3) | collective-permute-done | bytes 278560 | tf_op jit(solution)/shard_map/cond/branch_0_fun/ppermute | solution.py:223
  40.8 2.4 %collective-permute-done.2 = f32[544,128]{1,0:T(8,128)S(1)} collective-permute-done((f32[544,128]{1,0:T(8,128)S(1)}, f32[544,128]{1,0:T(8,128)S(1)}, u32[]{:S(2)}, u32[]{:S(2)}) %collective-permute-start.2) | collective-permute-done | bytes 278560 | tf_op jit(solution)/shard_map/cond/branch_0_fun/ppermute | solution.py:223
  45.4 2.1 %collective-permute-start.8 = (f32[544,128]{1,0:T(8,128)S(1)}, f32[544,128]{1,0:T(8,128)S(1)}, u32[]{:S(2)}, u32[]{:S(2)}) collective-permute-start(f32[544,128]{1,0:T(8,128)S(1)} %get-tuple-element.82), channel_id=1, source_target_pairs={{0,12},{1,0},{2,14},{3,2},{4,7},{5,1},{6,5},{7,3},{8,4},{9,8},{10,... | collective-permute-start | bytes 835592 | tf_op jit(solution)/shard_map/cond/branch_0_fun/ppermute | solution.py:223
  47.6 3.2 %collective-permute-start.10 = (f32[544,128]{1,0:T(8,128)S(1)}, f32[544,128]{1,0:T(8,128)S(1)}, u32[]{:S(2)}, u32[]{:S(2)}) collective-permute-start(f32[544,128]{1,0:T(8,128)S(1)} %get-tuple-element.80), channel_id=1, source_target_pairs={{0,2},{1,9},{2,0},{3,11},{4,12},{5,7},{6,14},{7,5},{8,10},{9,1},{1... | collective-permute-start | bytes 835592 | tf_op jit(solution)/shard_map/cond/branch_0_fun/ppermute | solution.py:223
  50.9 7.1 %collective-permute-done.6.r1 = f32[544,128]{1,0:T(8,128)S(1)} collective-permute-done((f32[544,128]{1,0:T(8,128)S(1)}, f32[544,128]{1,0:T(8,128)S(1)}, u32[]{:S(2)}, u32[]{:S(2)}) %collective-permute-start.6) | collective-permute-done | bytes 278560 | tf_op jit(solution)/shard_map/cond/branch_0_fun/ppermute | solution.py:223
  60.4 3.3 %collective-permute-start.23 = (f32[96,128]{1,0:T(8,128)S(1)}, f32[96,128]{1,0:T(8,128)S(1)}, u32[]{:S(2)}, u32[]{:S(2)}) collective-permute-start(f32[96,128]{1,0:T(8,128)S(1)} %get-tuple-element.98), channel_id=1, source_target_pairs={{0,8},{1,9},{2,10},{3,11},{4,12},{5,13},{6,14},{7,15},{8,0},{9,1},... | collective-permute-start | bytes 147464 | tf_op jit(solution)/shard_map/ppermute | solution.py:223
  64.8 1.5 %collective-permute-done.23 = f32[96,128]{1,0:T(8,128)S(1)} collective-permute-done((f32[96,128]{1,0:T(8,128)S(1)}, f32[96,128]{1,0:T(8,128)S(1)}, u32[]{:S(2)}, u32[]{:S(2)}) %collective-permute-start.23) | collective-permute-done | bytes 49184 | tf_op jit(solution)/shard_map/ppermute | solution.py:223
  66.3 1.5 %collective-permute-done.24 = f32[96,128]{1,0:T(8,128)S(1)} collective-permute-done((f32[96,128]{1,0:T(8,128)S(1)}, f32[96,128]{1,0:T(8,128)S(1)}, u32[]{:S(2)}, u32[]{:S(2)}) %collective-permute-start.24) | collective-permute-done | bytes 49184 | tf_op jit(solution)/shard_map/ppermute | solution.py:223
  67.8 3.3 %collective-permute-start.26 = (f32[384,128]{1,0:T(8,128)S(1)}, f32[384,128]{1,0:T(8,128)S(1)}, u32[]{:S(2)}, u32[]{:S(2)}) collective-permute-start(f32[384,128]{1,0:T(8,128)S(1)} %constant_dynamic-update-slice_fusion.refs_0_), channel_id=1, source_target_pairs={{0,2},{1,3},{2,0},{3,1},{4,6},{5,7},{6,4},{7,5},{8,10},{9,11},{10,... | collective-permute-start | bytes 589832 | tf_op jit(solution)/shard_map/ppermute | solution.py:223
  71.2 1.9 %collective-permute-start.27 = (f32[384,128]{1,0:T(8,128)S(1)}, f32[384,128]{1,0:T(8,128)S(1)}, u32[]{:S(2)}, u32[]{:S(2)}) collective-permute-start(f32[384,128]{1,0:T(8,128)S(1)} %constant_dynamic-update-slice_fusion.refs_0_), channel_id=1, source_target_pairs={{0,3},{1,0},{2,1},{3,2},{4,7},{5,4},{6,5},{7,6},{8,11},{9,8},{10,9... | collective-permute-start | bytes 589832 | tf_op jit(solution)/shard_map/ppermute | solution.py:223
  73.1 3.2 %halves.1 = (bf16[256,4096]{1,0:T(8,128)(2,1)S(1)}, bf16[256,4096]{1,0:T(8,128)(2,1)S(1)}) custom-call(f32[256,4096]{1,0:T(8,128)} %queries), custom_call_target="tpu_custom_call" | custom-call | flops 2097152 | bytes 8388608 | tf_op jit(solution)/shard_map/halves/pallas_call | solution.py:263
  76.3 1.5 %collective-permute-done.26.refs_2_ = f32[384,128]{1,0:T(8,128)S(1)} collective-permute-done((f32[384,128]{1,0:T(8,128)S(1)}, f32[384,128]{1,0:T(8,128)S(1)}, u32[]{:S(2)}, u32[]{:S(2)}) %collective-permute-start.26) | collective-permute-done | bytes 196640 | tf_op jit(solution)/shard_map/ppermute | solution.py:223
  77.8 2.2 %score.1 = (f32[48,256]{1,0:T(8,128)S(1)}, f32[8,256]{1,0:T(8,128)S(1)}) custom-call(s32[48]{0:T(128)S(1)} %get-tuple-element.79.segs, f32[384,128]{1,0:T(8,128)S(1)} %constant_dynamic-update-slice_fusion.refs_0_, f32[384,128]{1,0:T(8,128)S(1)} %collective-permute-done.25.refs_1_, f32[384,128]{1,0:T(8,128)S(1)} %collective-permute-done.26.refs_2_, ...), custom_call_target="tpu_custom_call" | custom-call | flops 301989888 | bytes 4194304 | tf_op jit(solution)/shard_map/score/pallas_call | solution.py:311
  81.2 3.0 %collective-permute-start.29 = (f32[8,256]{1,0:T(8,128)S(1)}, f32[8,256]{1,0:T(8,128)S(1)}, u32[]{:S(2)}, u32[]{:S(2)}) collective-permute-start(f32[8,256]{1,0:T(8,128)S(1)} %add.116), channel_id=1, source_target_pairs={{0,32},{16,48},{32,0},{48,16},{64,96},{80,112},{96,64},{112,80},{1... | collective-permute-start | bytes 24584 | tf_op jit(solution)/shard_map/ppermute | solution.py:357
  84.1 1.6 %collective-permute-done.29 = f32[8,256]{1,0:T(8,128)S(1)} collective-permute-done((f32[8,256]{1,0:T(8,128)S(1)}, f32[8,256]{1,0:T(8,128)S(1)}, u32[]{:S(2)}, u32[]{:S(2)}) %collective-permute-start.29) | collective-permute-done | bytes 8224 | tf_op jit(solution)/shard_map/ppermute | solution.py:357
  85.8 4.2 %collective-permute-start.30 = (f32[8,256]{1,0:T(8,128)S(1)}, f32[8,256]{1,0:T(8,128)S(1)}, u32[]{:S(2)}, u32[]{:S(2)}) collective-permute-start(f32[8,256]{1,0:T(8,128)S(1)} %add.117), channel_id=1, source_target_pairs={{0,96},{16,112},{32,64},{48,80},{64,32},{80,48},{96,0},{112,16},{1... | collective-permute-start | bytes 24584 | tf_op jit(solution)/shard_map/ppermute | solution.py:357
  89.9 1.6 %collective-permute-done.30 = f32[8,256]{1,0:T(8,128)S(1)} collective-permute-done((f32[8,256]{1,0:T(8,128)S(1)}, f32[8,256]{1,0:T(8,128)S(1)}, u32[]{:S(2)}, u32[]{:S(2)}) %collective-permute-start.30) | collective-permute-done | bytes 8224 | tf_op jit(solution)/shard_map/ppermute | solution.py:357
  (57 shorter events, 16.8 us)
Async XLA Ops:
  3.9 69.1 %copy-start.9 = (s32[48]{0:T(128)S(1)}, s32[48]{0:T(128)}, u32[]{:S(2)}) copy-start(s32[48]{0:T(128)} %param.20) | copy-start | bytes 580
  13.1 17.8 %collective-permute-start = (f32[1088,128]{1,0:T(8,128)}, f32[1088,128]{1,0:T(8,128)S(1)}, u32[]{:S(2)}, u32[]{:S(2)}) collective-permute-start(f32[1088,128]{1,0:T(8,128)} %get-tuple-element.39), channel_id=1, source_target_pairs={{0,1},{1,5},{2,3},{3,7},{4,0},{5,4},{6,2},{7,6},{8,9},{9,13},{10,1... | collective-permute-start | bytes 1671176 | tf_op jit(solution)/shard_map/cond/branch_0_fun/ppermute | solution.py:223
  14.9 16.1 %collective-permute-start.4 = (f32[1088,128]{1,0:T(8,128)}, f32[1088,128]{1,0:T(8,128)S(1)}, u32[]{:S(2)}, u32[]{:S(2)}) collective-permute-start(f32[1088,128]{1,0:T(8,128)} %get-tuple-element.43), channel_id=1, source_target_pairs={{0,3},{1,13},{2,1},{3,15},{4,8},{5,6},{6,10},{7,4},{8,11},{9,5},{1... | collective-permute-start | bytes 1671176 | tf_op jit(solution)/shard_map/cond/branch_0_fun/ppermute | solution.py:223
  18.2 15.4 %collective-permute-start.1 = (f32[1088,128]{1,0:T(8,128)}, f32[1088,128]{1,0:T(8,128)S(1)}, u32[]{:S(2)}, u32[]{:S(2)}) collective-permute-start(f32[1088,128]{1,0:T(8,128)} %get-tuple-element.41), channel_id=1, source_target_pairs={{0,4},{1,0},{2,6},{3,2},{4,5},{5,1},{6,7},{7,3},{8,12},{9,8},{10,1... | collective-permute-start | bytes 1671176 | tf_op jit(solution)/shard_map/cond/branch_0_fun/ppermute | solution.py:223
  18.2 15.4 %collective-permute-start.5 = (f32[1088,128]{1,0:T(8,128)}, f32[1088,128]{1,0:T(8,128)}, u32[]{:S(2)}, u32[]{:S(2)}) collective-permute-start(f32[1088,128]{1,0:T(8,128)} %get-tuple-element.44), channel_id=1, source_target_pairs={{0,12},{1,2},{2,14},{3,0},{4,7},{5,9},{6,5},{7,11},{8,4},{9,10},{1... | collective-permute-start | bytes 1671176 | tf_op jit(solution)/shard_map/cond/branch_0_fun/ppermute | solution.py:223
  30.9 16.6 %copy-start.6 = (f32[1088,128]{1,0:T(8,128)S(1)}, f32[1088,128]{1,0:T(8,128)}, u32[]{:S(2)}) copy-start(f32[1088,128]{1,0:T(8,128)} %get-tuple-element.38) | copy-start | bytes 1671172 | tf_op jit(solution)/shard_map/cond
  32.2 8.6 %collective-permute-start.3 = (f32[544,128]{1,0:T(8,128)S(1)}, f32[544,128]{1,0:T(8,128)S(1)}, u32[]{:S(2)}, u32[]{:S(2)}) collective-permute-start(f32[544,128]{1,0:T(8,128)S(1)} %get-tuple-element.87), channel_id=1, source_target_pairs={{0,12},{1,2},{2,14},{3,0},{4,7},{5,9},{6,5},{7,11},{8,4},{9,10},{1... | collective-permute-start | bytes 835592 | tf_op jit(solution)/shard_map/cond/branch_0_fun/ppermute | solution.py:223
  34.9 8.4 %collective-permute-start.2 = (f32[544,128]{1,0:T(8,128)S(1)}, f32[544,128]{1,0:T(8,128)S(1)}, u32[]{:S(2)}, u32[]{:S(2)}) collective-permute-start(f32[544,128]{1,0:T(8,128)S(1)} %get-tuple-element.85), channel_id=1, source_target_pairs={{0,3},{1,13},{2,1},{3,15},{4,8},{5,6},{6,10},{7,4},{8,11},{9,5},{1... | collective-permute-start | bytes 835592 | tf_op jit(solution)/shard_map/cond/branch_0_fun/ppermute | solution.py:223
  36.8 6.8 %collective-permute-start.7 = (f32[544,128]{1,0:T(8,128)S(1)}, f32[544,128]{1,0:T(8,128)S(1)}, u32[]{:S(2)}, u32[]{:S(2)}) collective-permute-start(f32[544,128]{1,0:T(8,128)S(1)} %get-tuple-element.86), channel_id=1, source_target_pairs={{0,4},{1,0},{2,6},{3,2},{4,5},{5,1},{6,7},{7,3},{8,12},{9,8},{10,1... | collective-permute-start | bytes 835592 | tf_op jit(solution)/shard_map/cond/branch_0_fun/ppermute | solution.py:223
  37.4 10.1 %collective-permute-start.9 = (f32[544,128]{1,0:T(8,128)S(1)}, f32[544,128]{1,0:T(8,128)S(1)}, u32[]{:S(2)}, u32[]{:S(2)}) collective-permute-start(f32[544,128]{1,0:T(8,128)S(1)} %get-tuple-element.84), channel_id=1, source_target_pairs={{0,1},{1,5},{2,3},{3,7},{4,0},{5,4},{6,2},{7,6},{8,9},{9,13},{10,1... | collective-permute-start | bytes 835592 | tf_op jit(solution)/shard_map/cond/branch_0_fun/ppermute | solution.py:223
  44.8 13.2 %collective-permute-start.6 = (f32[544,128]{1,0:T(8,128)S(1)}, f32[544,128]{1,0:T(8,128)S(1)}, u32[]{:S(2)}, u32[]{:S(2)}) collective-permute-start(f32[544,128]{1,0:T(8,128)S(1)} %get-tuple-element.83), channel_id=1, source_target_pairs={{0,4},{1,2},{2,6},{3,0},{4,5},{5,9},{6,7},{7,11},{8,12},{9,10},{10... | collective-permute-start | bytes 835592 | tf_op jit(solution)/shard_map/cond/branch_0_fun/ppermute | solution.py:223
  45.4 12.5 %collective-permute-start.8 = (f32[544,128]{1,0:T(8,128)S(1)}, f32[544,128]{1,0:T(8,128)S(1)}, u32[]{:S(2)}, u32[]{:S(2)}) collective-permute-start(f32[544,128]{1,0:T(8,128)S(1)} %get-tuple-element.82), channel_id=1, source_target_pairs={{0,12},{1,0},{2,14},{3,2},{4,7},{5,1},{6,5},{7,3},{8,4},{9,8},{10,... | collective-permute-start | bytes 835592 | tf_op jit(solution)/shard_map/cond/branch_0_fun/ppermute | solution.py:223
  47.6 10.4 %collective-permute-start.10 = (f32[544,128]{1,0:T(8,128)S(1)}, f32[544,128]{1,0:T(8,128)S(1)}, u32[]{:S(2)}, u32[]{:S(2)}) collective-permute-start(f32[544,128]{1,0:T(8,128)S(1)} %get-tuple-element.80), channel_id=1, source_target_pairs={{0,2},{1,9},{2,0},{3,11},{4,12},{5,7},{6,14},{7,5},{8,10},{9,1},{1... | collective-permute-start | bytes 835592 | tf_op jit(solution)/shard_map/cond/branch_0_fun/ppermute | solution.py:223
  59.4 18.4 %copy-start = (s32[16,16]{1,0:T(8,128)S(1)}, s32[16,16]{1,0:T(8,128)}, u32[]{:S(2)}) copy-start(s32[16,16]{1,0:T(8,128)} %refs_8_.1) | copy-start | bytes 3076
  59.4 18.4 %copy-start.1 = (s32[256]{0:T(256)S(1)}, s32[256]{0:T(256)}, u32[]{:S(2)}) copy-start(s32[256]{0:T(256)} %param.21) | copy-start | bytes 3076
  59.4 5.4 %collective-permute-start.22 = (f32[96,128]{1,0:T(8,128)S(1)}, f32[96,128]{1,0:T(8,128)S(1)}, u32[]{:S(2)}, u32[]{:S(2)}) collective-permute-start(f32[96,128]{1,0:T(8,128)S(1)} %get-tuple-element.98), channel_id=1, source_target_pairs={{0,4},{1,5},{2,6},{3,7},{4,8},{5,9},{6,10},{7,11},{8,12},{9,13},{1... | collective-permute-start | bytes 147464 | tf_op jit(solution)/shard_map/ppermute | solution.py:223
  60.4 5.9 %collective-permute-start.23 = (f32[96,128]{1,0:T(8,128)S(1)}, f32[96,128]{1,0:T(8,128)S(1)}, u32[]{:S(2)}, u32[]{:S(2)}) collective-permute-start(f32[96,128]{1,0:T(8,128)S(1)} %get-tuple-element.98), channel_id=1, source_target_pairs={{0,8},{1,9},{2,10},{3,11},{4,12},{5,13},{6,14},{7,15},{8,0},{9,1},... | collective-permute-start | bytes 147464 | tf_op jit(solution)/shard_map/ppermute | solution.py:223
  63.7 4.1 %collective-permute-start.24 = (f32[96,128]{1,0:T(8,128)S(1)}, f32[96,128]{1,0:T(8,128)S(1)}, u32[]{:S(2)}, u32[]{:S(2)}) collective-permute-start(f32[96,128]{1,0:T(8,128)S(1)} %get-tuple-element.98), channel_id=1, source_target_pairs={{0,12},{1,13},{2,14},{3,15},{4,0},{5,1},{6,2},{7,3},{8,4},{9,5},{1... | collective-permute-start | bytes 147464 | tf_op jit(solution)/shard_map/ppermute | solution.py:223
  67.8 8.5 %collective-permute-start.25 = (f32[384,128]{1,0:T(8,128)S(1)}, f32[384,128]{1,0:T(8,128)S(1)}, u32[]{:S(2)}, u32[]{:S(2)}) collective-permute-start(f32[384,128]{1,0:T(8,128)S(1)} %constant_dynamic-update-slice_fusion.refs_0_), channel_id=1, source_target_pairs={{0,1},{1,2},{2,3},{3,0},{4,5},{5,6},{6,7},{7,4},{8,9},{9,10},{10,1... | collective-permute-start | bytes 589832 | tf_op jit(solution)/shard_map/ppermute | solution.py:223
  67.8 9.9 %collective-permute-start.26 = (f32[384,128]{1,0:T(8,128)S(1)}, f32[384,128]{1,0:T(8,128)S(1)}, u32[]{:S(2)}, u32[]{:S(2)}) collective-permute-start(f32[384,128]{1,0:T(8,128)S(1)} %constant_dynamic-update-slice_fusion.refs_0_), channel_id=1, source_target_pairs={{0,2},{1,3},{2,0},{3,1},{4,6},{5,7},{6,4},{7,5},{8,10},{9,11},{10,... | collective-permute-start | bytes 589832 | tf_op jit(solution)/shard_map/ppermute | solution.py:223
  71.2 6.6 %collective-permute-start.27 = (f32[384,128]{1,0:T(8,128)S(1)}, f32[384,128]{1,0:T(8,128)S(1)}, u32[]{:S(2)}, u32[]{:S(2)}) collective-permute-start(f32[384,128]{1,0:T(8,128)S(1)} %constant_dynamic-update-slice_fusion.refs_0_), channel_id=1, source_target_pairs={{0,3},{1,0},{2,1},{3,2},{4,7},{5,4},{6,5},{7,6},{8,11},{9,8},{10,9... | collective-permute-start | bytes 589832 | tf_op jit(solution)/shard_map/ppermute | solution.py:223
  79.9 1.3 %collective-permute-start.28 = (f32[8,256]{1,0:T(8,128)S(1)}, f32[8,256]{1,0:T(8,128)S(1)}, u32[]{:S(2)}, u32[]{:S(2)}) collective-permute-start(f32[8,256]{1,0:T(8,128)S(1)} %get-tuple-element.75), channel_id=1, source_target_pairs={{0,16},{16,0},{32,48},{48,32},{64,80},{80,64},{96,112},{112,96},{1... | collective-permute-start | bytes 24584 | tf_op jit(solution)/shard_map/ppermute | solution.py:357
  81.2 4.6 %collective-permute-start.29 = (f32[8,256]{1,0:T(8,128)S(1)}, f32[8,256]{1,0:T(8,128)S(1)}, u32[]{:S(2)}, u32[]{:S(2)}) collective-permute-start(f32[8,256]{1,0:T(8,128)S(1)} %add.116), channel_id=1, source_target_pairs={{0,32},{16,48},{32,0},{48,16},{64,96},{80,112},{96,64},{112,80},{1... | collective-permute-start | bytes 24584 | tf_op jit(solution)/shard_map/ppermute | solution.py:357
  85.8 5.8 %collective-permute-start.30 = (f32[8,256]{1,0:T(8,128)S(1)}, f32[8,256]{1,0:T(8,128)S(1)}, u32[]{:S(2)}, u32[]{:S(2)}) collective-permute-start(f32[8,256]{1,0:T(8,128)S(1)} %add.117), channel_id=1, source_target_pairs={{0,96},{16,112},{32,64},{48,80},{64,32},{80,48},{96,0},{112,16},{1... | collective-permute-start | bytes 24584 | tf_op jit(solution)/shard_map/ppermute | solution.py:357
  (4 other events, 64.3 us)
where the time goes:
time: 92.2 us
  starting transfers between devices  35.3 us (38%)
  Pallas kernels  26.5 us (29%)
  waiting for transfers between devices  21.4 us (23%)
  other arithmetic  6.95 us (8%)
  local copies, waits for them, and re-layouts  0.95 us (1%)
    ppermute x17, starting transfers between devices, hop(): return lax.ppermute(x, 'rank', pairs)  28.1 us
    pallas_call x2, Pallas kernels, project(): pl.pallas_call(functools.partial(project_kernel, part * n), in_specs=[sme...  20 us
    ppermute x17, waiting for transfers between devices, hop(): return lax.ppermute(x, 'rank', pairs)  17 us
    ppermute x3, starting transfers between devices, per_device(): total = total + lax.ppermute(total, 'dp', other)  7.2 us
    ppermute x3, waiting for transfers between devices, per_device(): total = total + lax.ppermute(total, 'dp', other)  4.41 us
    pallas_call x1, Pallas kernels, halves(): pl.pallas_call(halves_kernel, grid=(steps,), in_specs=[spec], out_specs=[...  3.16 us
    add x2, other arithmetic, features(): onward[home, stream] = at_b + got[home, stream][cap:]  2.42 us
    pallas_call x1, Pallas kernels, score(): pl.pallas_call(score_kernel, in_specs=[pl.BlockSpec(memory_space=pltpu.SM...  2.15 us
  transfers between devices with their start and end apart: 20, of which 11 were waited for; matrix products, arithmetic and copies ran while one was open for 4% of the time, Pallas kernels for 15%

commit v1 on v0

--- a/solution.py
+++ b/solution.py
@@ -92,7 +92,7 @@
 
 
 def project_kernel(first, segs, cnts, acts, grads, w_in, w_out, *refs):
-    outs, (act_buf, grad_buf, spill, sems) = refs[:4], refs[4:]
+    outs, (act_buf, grad_buf, made_buf, spill, sems, out_sems) = refs[:4], refs[4:]
     toks = act_buf.shape[1]
     cap = outs[0].shape[0] // 2
 
@@ -114,7 +114,9 @@
         side_a = lax.dot_general(act_buf[j], w_a, nt, preferred_element_type=F32)
         return side_a + jnp.concatenate([side_g, jnp.zeros_like(side_g)], axis=0).T
 
-    for h, out in enumerate(outs):
+    leaving = []
+    for h in range(len(outs)):
+        out = made_buf.at[h]
 
         def block(i, _):
             j = (h * 2 + i) * SLOTS
@@ -137,6 +139,10 @@
             return lax.fori_loop(0, up(cnts[first + j + 2], 16) // 16, piece, 0)
 
         lax.fori_loop(0, 2, block, 0)
+        leaving.append(pltpu.make_async_copy(out, outs[h], out_sems.at[h]))
+        leaving[-1].start()
+    for copy in leaving:
+        copy.wait()
 
 
 def project(part, cap, segs, cnts, acts, grads_t, w_in, w_out):
@@ -149,15 +155,17 @@
     return pl.pallas_call(
         functools.partial(project_kernel, part * n),
         in_specs=[smem, smem, any_, any_, vmem, vmem],
-        out_specs=[vmem] * 4,
+        out_specs=[any_] * 4,
         out_shape=[jax.ShapeDtypeStruct((2 * cap, 128), F32)] * 4,
         scratch_shapes=[
             pltpu.VMEM((n, toks, fa), BF16),
             pltpu.VMEM((n, fg, toks), BF16),
+            pltpu.VMEM((4, 2 * cap, 128), F32),
             pltpu.VMEM((toks, 128), F32),
             pltpu.SemaphoreType.DMA((n, 2)),
+            pltpu.SemaphoreType.DMA((4,)),
         ],
-        compiler_params=pltpu.CompilerParams(vmem_limit_bytes=56 * 2**20),
+        compiler_params=pltpu.CompilerParams(vmem_limit_bytes=40 * 2**20),
         cost_estimate=pl.CostEstimate(
             flops=n * toks * 2 * 64 * (fa + fg),
             bytes_accessed=n * toks * 2 * (fa + fg) + 8 * cap * 512,

time: 92.2 us -> 86.9 us (0.943)
  other arithmetic: 6.95 us -> 3.45 us
  Pallas kernels: 26.5 us -> 23.5 us
  waiting for transfers between devices: 21.4 us -> 23.9 us
  starting transfers between devices: 35.3 us -> 33.4 us
    pallas_call x2, Pallas kernels: 20 us -> 17.1 us  [project(): pl.pallas_call(functools.partial(project_kernel, part * n), in_specs=[sme...]
    add x2, other arithmetic: 2.42 us -> 0.11 us  [features(): onward[home, stream] = at_b + got[home, stream][cap:]]
    ppermute x17, waiting for transfers between devices: 17 us -> 19.3 us  [hop(): return lax.ppermute(x, 'rank', pairs)]
    ppermute x3, starting transfers between devices: 7.2 us -> 5.49 us  [per_device(): total = total + lax.ppermute(total, 'dp', other)]
    add x2, other arithmetic: 1.35 us -> 0.15 us  [features(): done[home, stream] = stay + got[home, stream][:cap] + came[home, stream]]
  transfers between devices with their start and end apart: 20 -> 20, of which waited for: 11 -> 13; matrix products, arithmetic and copies ran while one was open for 4% -> 1% of each run, Pallas kernels for 15% -> 14%
where the time goes in v1:
time: 86.9 us; the launch traced here: 86.3 us
  starting transfers between devices  33.4 us (38%)
  waiting for transfers between devices  23.9 us (28%)
  Pallas kernels  23.5 us (27%)
  other arithmetic  3.45 us (4%)
  local copies, waits for them, and re-layouts  0.94 us (1%)
    ppermute x17, starting transfers between devices, hop(): return lax.ppermute(x, 'rank', pairs)  27.9 us
    ppermute x17, waiting for transfers between devices, hop(): return lax.ppermute(x, 'rank', pairs)  19.3 us
    pallas_call x2, Pallas kernels, project(): pl.pallas_call(functools.partial(project_kernel, part * n), in_specs=[sme...  17.1 us
    ppermute x3, starting transfers between devices, per_device(): total = total + lax.ppermute(total, 'dp', other)  5.49 us
    ppermute x3, waiting for transfers between devices, per_device(): total = total + lax.ppermute(total, 'dp', other)  4.62 us
    pallas_call x1, Pallas kernels, halves(): pl.pallas_call(halves_kernel, grid=(steps,), in_specs=[spec], out_specs=[...  3.16 us
    pallas_call x1, Pallas kernels, score(): pl.pallas_call(score_kernel, in_specs=[pl.BlockSpec(memory_space=pltpu.SM...  2.15 us
  transfers between devices with their start and end apart: 20, of which 13 were waited for; matrix products, arithmetic and copies ran while one was open for 1% of the time, Pallas kernels for 14%

profile of v1, /device:TPU:0, one launch (start us, length us, event | category | flops | bytes accessed | tf_op | source)
XLA Modules:
  0.0 86.3 jit_solution(16331000453419778950)
XLA Ops:
  3.9 51.0 %conditional.1 = (f32[96,128]{1,0:T(8,128)S(1)}) conditional(s32[]{:T(128)} %clamp.8, (s32[48]{0:T(128)S(1)}, s32[48]{0:T(128)S(1)}, bf16[48,256,256]{2,1,0:T(8,128)(2,1)}, bf16[48,688,256]{2,1,0:T(8,128)(2,1)}, bf16[64,256]{1,0:T(8,128)(2,1)}, /*index=5*/bf16[64,688]{1,0:T(8,128)(2,1)}) %tuple.34, (s32[48]{0:T(128)S(1)}, s32[48]{0:T(128)S(1)}, ...), branch_computations={%region_6.7_spmd, %region_7.8_spmd} | conditional | flops 1599209472 | bytes 133784112 | solution.py:354
  4.0 8.1 %project.5 = (f32[1088,128]{1,0:T(8,128)S(1)}, f32[1088,128]{1,0:T(8,128)S(1)}, f32[1088,128]{1,0:T(8,128)S(1)}, f32[1088,128]{1,0:T(8,128)S(1)}) custom-call(s32[48]{0:T(128)S(1)} %get-tuple-element.33.segs, s32[48]{0:T(128)S(1)} %get-tuple-element.32.cnts, bf16[48,256,256]{2,1,0:T(8,128)(2,1)} %get-tuple-element.34.acts, ...), custom_call_target="tpu_custom_call" | custom-call | flops 742391808 | bytes 13828096 | tf_op jit(solution)/shard_map/cond/branch_0_fun/project/pallas_call | solution.py:155
  12.0 1.9 %collective-permute-start = (f32[1088,128]{1,0:T(8,128)S(1)}, f32[1088,128]{1,0:T(8,128)S(1)}, u32[]{:S(2)}, u32[]{:S(2)}) collective-permute-start(f32[1088,128]{1,0:T(8,128)S(1)} %get-tuple-element.39), channel_id=1, source_target_pairs={{0,1},{1,5},{2,3},{3,7},{4,0},{5,4},{6,2},{7,6},{8,9},{9,13},{10,1... | collective-permute-start | bytes 1671176 | tf_op jit(solution)/shard_map/cond/branch_0_fun/ppermute | solution.py:231
  14.0 2.7 %collective-permute-start.4 = (f32[1088,128]{1,0:T(8,128)S(1)}, f32[1088,128]{1,0:T(8,128)S(1)}, u32[]{:S(2)}, u32[]{:S(2)}) collective-permute-start(f32[1088,128]{1,0:T(8,128)S(1)} %get-tuple-element.43), channel_id=1, source_target_pairs={{0,3},{1,13},{2,1},{3,15},{4,8},{5,6},{6,10},{7,4},{8,11},{9,5},{1... | collective-permute-start | bytes 1671176 | tf_op jit(solution)/shard_map/cond/branch_0_fun/ppermute | solution.py:231
  16.8 2.2 %collective-permute-start.5 = (f32[1088,128]{1,0:T(8,128)S(1)}, f32[1088,128]{1,0:T(8,128)S(1)}, u32[]{:S(2)}, u32[]{:S(2)}) collective-permute-start(f32[1088,128]{1,0:T(8,128)S(1)} %get-tuple-element.44), channel_id=1, source_target_pairs={{0,12},{1,2},{2,14},{3,0},{4,7},{5,9},{6,5},{7,11},{8,4},{9,10},{1... | collective-permute-start | bytes 1671176 | tf_op jit(solution)/shard_map/cond/branch_0_fun/ppermute | solution.py:231
  18.9 9.0 %project.4 = (f32[1088,128]{1,0:T(8,128)S(1)}, f32[1088,128]{1,0:T(8,128)S(1)}, f32[1088,128]{1,0:T(8,128)S(1)}, f32[1088,128]{1,0:T(8,128)S(1)}) custom-call(s32[48]{0:T(128)S(1)} %get-tuple-element.33.segs, s32[48]{0:T(128)S(1)} %get-tuple-element.32.cnts, bf16[48,256,256]{2,1,0:T(8,128)(2,1)} %get-tuple-element.34.acts, ...), custom_call_target="tpu_custom_call" | custom-call | flops 742391808 | bytes 13828096 | tf_op jit(solution)/shard_map/cond/branch_0_fun/project/pallas_call | solution.py:155
  29.1 2.1 %collective-permute-start.3 = (f32[544,128]{1,0:T(8,128)S(1)}, f32[544,128]{1,0:T(8,128)S(1)}, u32[]{:S(2)}, u32[]{:S(2)}) collective-permute-start(f32[544,128]{1,0:T(8,128)S(1)} %get-tuple-element.87), channel_id=1, source_target_pairs={{0,12},{1,2},{2,14},{3,0},{4,7},{5,9},{6,5},{7,11},{8,4},{9,10},{1... | collective-permute-start | bytes 835592 | tf_op jit(solution)/shard_map/cond/branch_0_fun/ppermute | solution.py:231
  31.8 2.0 %collective-permute-start.2 = (f32[544,128]{1,0:T(8,128)S(1)}, f32[544,128]{1,0:T(8,128)S(1)}, u32[]{:S(2)}, u32[]{:S(2)}) collective-permute-start(f32[544,128]{1,0:T(8,128)S(1)} %get-tuple-element.85), channel_id=1, source_target_pairs={{0,3},{1,13},{2,1},{3,15},{4,8},{5,6},{6,10},{7,4},{8,11},{9,5},{1... | collective-permute-start | bytes 835592 | tf_op jit(solution)/shard_map/cond/branch_0_fun/ppermute | solution.py:231
  34.6 1.3 %collective-permute-start.9 = (f32[544,128]{1,0:T(8,128)S(1)}, f32[544,128]{1,0:T(8,128)S(1)}, u32[]{:S(2)}, u32[]{:S(2)}) collective-permute-start(f32[544,128]{1,0:T(8,128)S(1)} %get-tuple-element.84), channel_id=1, source_target_pairs={{0,1},{1,5},{2,3},{3,7},{4,0},{5,4},{6,2},{7,6},{8,9},{9,13},{10,1... | collective-permute-start | bytes 835592 | tf_op jit(solution)/shard_map/cond/branch_0_fun/ppermute | solution.py:231
  35.9 1.8 %collective-permute-done.3 = f32[544,128]{1,0:T(8,128)S(1)} collective-permute-done((f32[544,128]{1,0:T(8,128)S(1)}, f32[544,128]{1,0:T(8,128)S(1)}, u32[]{:S(2)}, u32[]{:S(2)}) %collective-permute-start.3) | collective-permute-done | bytes 278560 | tf_op jit(solution)/shard_map/cond/branch_0_fun/ppermute | solution.py:231
  37.7 2.2 %collective-permute-done.2 = f32[544,128]{1,0:T(8,128)S(1)} collective-permute-done((f32[544,128]{1,0:T(8,128)S(1)}, f32[544,128]{1,0:T(8,128)S(1)}, u32[]{:S(2)}, u32[]{:S(2)}) %collective-permute-start.2) | collective-permute-done | bytes 278560 | tf_op jit(solution)/shard_map/cond/branch_0_fun/ppermute | solution.py:231
  41.3 1.6 %collective-permute-start.8 = (f32[544,128]{1,0:T(8,128)S(1)}, f32[544,128]{1,0:T(8,128)S(1)}, u32[]{:S(2)}, u32[]{:S(2)}) collective-permute-start(f32[544,128]{1,0:T(8,128)S(1)} %get-tuple-element.82), channel_id=1, source_target_pairs={{0,12},{1,0},{2,14},{3,2},{4,7},{5,1},{6,5},{7,3},{8,4},{9,8},{10,... | collective-permute-start | bytes 835592 | tf_op jit(solution)/shard_map/cond/branch_0_fun/ppermute | solution.py:231
  43.1 2.9 %collective-permute-start.10 = (f32[544,128]{1,0:T(8,128)S(1)}, f32[544,128]{1,0:T(8,128)S(1)}, u32[]{:S(2)}, u32[]{:S(2)}) collective-permute-start(f32[544,128]{1,0:T(8,128)S(1)} %get-tuple-element.80), channel_id=1, source_target_pairs={{0,2},{1,9},{2,0},{3,11},{4,12},{5,7},{6,14},{7,5},{8,10},{9,1},{1... | collective-permute-start | bytes 835592 | tf_op jit(solution)/shard_map/cond/branch_0_fun/ppermute | solution.py:231
  46.0 7.5 %collective-permute-done.6.r1 = f32[544,128]{1,0:T(8,128)S(1)} collective-permute-done((f32[544,128]{1,0:T(8,128)S(1)}, f32[544,128]{1,0:T(8,128)S(1)}, u32[]{:S(2)}, u32[]{:S(2)}) %collective-permute-start.6) | collective-permute-done | bytes 278560 | tf_op jit(solution)/shard_map/cond/branch_0_fun/ppermute | solution.py:231
  55.4 3.4 %collective-permute-start.23 = (f32[96,128]{1,0:T(8,128)S(1)}, f32[96,128]{1,0:T(8,128)S(1)}, u32[]{:S(2)}, u32[]{:S(2)}) collective-permute-start(f32[96,128]{1,0:T(8,128)S(1)} %get-tuple-element.98), channel_id=1, source_target_pairs={{0,8},{1,9},{2,10},{3,11},{4,12},{5,13},{6,14},{7,15},{8,0},{9,1},... | collective-permute-start | bytes 147464 | tf_op jit(solution)/shard_map/ppermute | solution.py:231
  61.3 1.5 %collective-permute-done.24 = f32[96,128]{1,0:T(8,128)S(1)} collective-permute-done((f32[96,128]{1,0:T(8,128)S(1)}, f32[96,128]{1,0:T(8,128)S(1)}, u32[]{:S(2)}, u32[]{:S(2)}) %collective-permute-start.24) | collective-permute-done | bytes 49184 | tf_op jit(solution)/shard_map/ppermute | solution.py:231
  62.9 3.9 %collective-permute-start.26 = (f32[384,128]{1,0:T(8,128)S(1)}, f32[384,128]{1,0:T(8,128)S(1)}, u32[]{:S(2)}, u32[]{:S(2)}) collective-permute-start(f32[384,128]{1,0:T(8,128)S(1)} %constant_dynamic-update-slice_fusion.refs_0_), channel_id=1, source_target_pairs={{0,2},{1,3},{2,0},{3,1},{4,6},{5,7},{6,4},{7,5},{8,10},{9,11},{10,... | collective-permute-start | bytes 589832 | tf_op jit(solution)/shard_map/ppermute | solution.py:231
  68.1 3.2 %halves.1 = (bf16[256,4096]{1,0:T(8,128)(2,1)S(1)}, bf16[256,4096]{1,0:T(8,128)(2,1)S(1)}) custom-call(f32[256,4096]{1,0:T(8,128)} %queries), custom_call_target="tpu_custom_call" | custom-call | flops 2097152 | bytes 8388608 | tf_op jit(solution)/shard_map/halves/pallas_call | solution.py:271
  71.3 2.1 %collective-permute-done.26.refs_2_ = f32[384,128]{1,0:T(8,128)S(1)} collective-permute-done((f32[384,128]{1,0:T(8,128)S(1)}, f32[384,128]{1,0:T(8,128)S(1)}, u32[]{:S(2)}, u32[]{:S(2)}) %collective-permute-start.26) | collective-permute-done | bytes 196640 | tf_op jit(solution)/shard_map/ppermute | solution.py:231
  73.4 2.1 %score.1 = (f32[48,256]{1,0:T(8,128)S(1)}, f32[8,256]{1,0:T(8,128)S(1)}) custom-call(s32[48]{0:T(128)S(1)} %get-tuple-element.79.segs, f32[384,128]{1,0:T(8,128)S(1)} %constant_dynamic-update-slice_fusion.refs_0_, f32[384,128]{1,0:T(8,128)S(1)} %collective-permute-done.25.refs_1_, f32[384,128]{1,0:T(8,128)S(1)} %collective-permute-done.26.refs_2_, ...), custom_call_target="tpu_custom_call" | custom-call | flops 301989888 | bytes 4194304 | tf_op jit(solution)/shard_map/score/pallas_call | solution.py:319
  76.8 2.4 %collective-permute-start.29 = (f32[8,256]{1,0:T(8,128)S(1)}, f32[8,256]{1,0:T(8,128)S(1)}, u32[]{:S(2)}, u32[]{:S(2)}) collective-permute-start(f32[8,256]{1,0:T(8,128)S(1)} %add.116), channel_id=1, source_target_pairs={{0,32},{16,48},{32,0},{48,16},{64,96},{80,112},{96,64},{112,80},{1... | collective-permute-start | bytes 24584 | tf_op jit(solution)/shard_map/ppermute | solution.py:365
  79.2 1.6 %collective-permute-done.29 = f32[8,256]{1,0:T(8,128)S(1)} collective-permute-done((f32[8,256]{1,0:T(8,128)S(1)}, f32[8,256]{1,0:T(8,128)S(1)}, u32[]{:S(2)}, u32[]{:S(2)}) %collective-permute-start.29) | collective-permute-done | bytes 8224 | tf_op jit(solution)/shard_map/ppermute | solution.py:365
  80.8 3.0 %collective-permute-start.30 = (f32[8,256]{1,0:T(8,128)S(1)}, f32[8,256]{1,0:T(8,128)S(1)}, u32[]{:S(2)}, u32[]{:S(2)}) collective-permute-start(f32[8,256]{1,0:T(8,128)S(1)} %add.117), channel_id=1, source_target_pairs={{0,96},{16,112},{32,64},{48,80},{64,32},{80,48},{96,0},{112,16},{1... | collective-permute-start | bytes 24584 | tf_op jit(solution)/shard_map/ppermute | solution.py:365
  83.8 1.8 %collective-permute-done.30 = f32[8,256]{1,0:T(8,128)S(1)} collective-permute-done((f32[8,256]{1,0:T(8,128)S(1)}, f32[8,256]{1,0:T(8,128)S(1)}, u32[]{:S(2)}, u32[]{:S(2)}) %collective-permute-start.30) | collective-permute-done | bytes 8224 | tf_op jit(solution)/shard_map/ppermute | solution.py:365
  (52 shorter events, 14.9 us)
Async XLA Ops:
  3.9 64.1 %copy-start.8 = (s32[48]{0:T(128)S(1)}, s32[48]{0:T(128)}, u32[]{:S(2)}) copy-start(s32[48]{0:T(128)} %param.20) | copy-start | bytes 580
  3.9 15.0 %copy-start.2 = (bf16[48,688,256]{2,1,0:T(8,128)(2,1)S(1)}, bf16[48,688,256]{2,1,0:T(8,128)(2,1)}, u32[]{:S(2)}) copy-start(bf16[48,688,256]{2,1,0:T(8,128)(2,1)} %get-tuple-element.35.grads) | copy-start | bytes 50724868 | tf_op jit(solution)/shard_map/cond
  12.0 15.9 %collective-permute-start = (f32[1088,128]{1,0:T(8,128)S(1)}, f32[1088,128]{1,0:T(8,128)S(1)}, u32[]{:S(2)}, u32[]{:S(2)}) collective-permute-start(f32[1088,128]{1,0:T(8,128)S(1)} %get-tuple-element.39), channel_id=1, source_target_pairs={{0,1},{1,5},{2,3},{3,7},{4,0},{5,4},{6,2},{7,6},{8,9},{9,13},{10,1... | collective-permute-start | bytes 1671176 | tf_op jit(solution)/shard_map/cond/branch_0_fun/ppermute | solution.py:231
  14.0 15.1 %collective-permute-start.4 = (f32[1088,128]{1,0:T(8,128)S(1)}, f32[1088,128]{1,0:T(8,128)S(1)}, u32[]{:S(2)}, u32[]{:S(2)}) collective-permute-start(f32[1088,128]{1,0:T(8,128)S(1)} %get-tuple-element.43), channel_id=1, source_target_pairs={{0,3},{1,13},{2,1},{3,15},{4,8},{5,6},{6,10},{7,4},{8,11},{9,5},{1... | collective-permute-start | bytes 1671176 | tf_op jit(solution)/shard_map/cond/branch_0_fun/ppermute | solution.py:231
  16.7 14.5 %collective-permute-start.1 = (f32[1088,128]{1,0:T(8,128)S(1)}, f32[1088,128]{1,0:T(8,128)S(1)}, u32[]{:S(2)}, u32[]{:S(2)}) collective-permute-start(f32[1088,128]{1,0:T(8,128)S(1)} %get-tuple-element.41), channel_id=1, source_target_pairs={{0,4},{1,0},{2,6},{3,2},{4,5},{5,1},{6,7},{7,3},{8,12},{9,8},{10,1... | collective-permute-start | bytes 1671176 | tf_op jit(solution)/shard_map/cond/branch_0_fun/ppermute | solution.py:231
  16.8 15.0 %collective-permute-start.5 = (f32[1088,128]{1,0:T(8,128)S(1)}, f32[1088,128]{1,0:T(8,128)S(1)}, u32[]{:S(2)}, u32[]{:S(2)}) collective-permute-start(f32[1088,128]{1,0:T(8,128)S(1)} %get-tuple-element.44), channel_id=1, source_target_pairs={{0,12},{1,2},{2,14},{3,0},{4,7},{5,9},{6,5},{7,11},{8,4},{9,10},{1... | collective-permute-start | bytes 1671176 | tf_op jit(solution)/shard_map/cond/branch_0_fun/ppermute | solution.py:231
  29.1 8.6 %collective-permute-start.3 = (f32[544,128]{1,0:T(8,128)S(1)}, f32[544,128]{1,0:T(8,128)S(1)}, u32[]{:S(2)}, u32[]{:S(2)}) collective-permute-start(f32[544,128]{1,0:T(8,128)S(1)} %get-tuple-element.87), channel_id=1, source_target_pairs={{0,12},{1,2},{2,14},{3,0},{4,7},{5,9},{6,5},{7,11},{8,4},{9,10},{1... | collective-permute-start | bytes 835592 | tf_op jit(solution)/shard_map/cond/branch_0_fun/ppermute | solution.py:231
  31.8 8.1 %collective-permute-start.2 = (f32[544,128]{1,0:T(8,128)S(1)}, f32[544,128]{1,0:T(8,128)S(1)}, u32[]{:S(2)}, u32[]{:S(2)}) collective-permute-start(f32[544,128]{1,0:T(8,128)S(1)} %get-tuple-element.85), channel_id=1, source_target_pairs={{0,3},{1,13},{2,1},{3,15},{4,8},{5,6},{6,10},{7,4},{8,11},{9,5},{1... | collective-permute-start | bytes 835592 | tf_op jit(solution)/shard_map/cond/branch_0_fun/ppermute | solution.py:231
  33.8 6.6 %collective-permute-start.7 = (f32[544,128]{1,0:T(8,128)S(1)}, f32[544,128]{1,0:T(8,128)S(1)}, u32[]{:S(2)}, u32[]{:S(2)}) collective-permute-start(f32[544,128]{1,0:T(8,128)S(1)} %get-tuple-element.86), channel_id=1, source_target_pairs={{0,4},{1,0},{2,6},{3,2},{4,5},{5,1},{6,7},{7,3},{8,12},{9,8},{10,1... | collective-permute-start | bytes 835592 | tf_op jit(solution)/shard_map/cond/branch_0_fun/ppermute | solution.py:231
  34.6 8.4 %collective-permute-start.9 = (f32[544,128]{1,0:T(8,128)S(1)}, f32[544,128]{1,0:T(8,128)S(1)}, u32[]{:S(2)}, u32[]{:S(2)}) collective-permute-start(f32[544,128]{1,0:T(8,128)S(1)} %get-tuple-element.84), channel_id=1, source_target_pairs={{0,1},{1,5},{2,3},{3,7},{4,0},{5,4},{6,2},{7,6},{8,9},{9,13},{10,1... | collective-permute-start | bytes 835592 | tf_op jit(solution)/shard_map/cond/branch_0_fun/ppermute | solution.py:231
  40.6 13.0 %collective-permute-start.6 = (f32[544,128]{1,0:T(8,128)S(1)}, f32[544,128]{1,0:T(8,128)S(1)}, u32[]{:S(2)}, u32[]{:S(2)}) collective-permute-start(f32[544,128]{1,0:T(8,128)S(1)} %get-tuple-element.83), channel_id=1, source_target_pairs={{0,4},{1,2},{2,6},{3,0},{4,5},{5,9},{6,7},{7,11},{8,12},{9,10},{10... | collective-permute-start | bytes 835592 | tf_op jit(solution)/shard_map/cond/branch_0_fun/ppermute | solution.py:231
  41.3 12.2 %collective-permute-start.8 = (f32[544,128]{1,0:T(8,128)S(1)}, f32[544,128]{1,0:T(8,128)S(1)}, u32[]{:S(2)}, u32[]{:S(2)}) collective-permute-start(f32[544,128]{1,0:T(8,128)S(1)} %get-tuple-element.82), channel_id=1, source_target_pairs={{0,12},{1,0},{2,14},{3,2},{4,7},{5,1},{6,5},{7,3},{8,4},{9,8},{10,... | collective-permute-start | bytes 835592 | tf_op jit(solution)/shard_map/cond/branch_0_fun/ppermute | solution.py:231
  43.1 10.5 %collective-permute-start.10 = (f32[544,128]{1,0:T(8,128)S(1)}, f32[544,128]{1,0:T(8,128)S(1)}, u32[]{:S(2)}, u32[]{:S(2)}) collective-permute-start(f32[544,128]{1,0:T(8,128)S(1)} %get-tuple-element.80), channel_id=1, source_target_pairs={{0,2},{1,9},{2,0},{3,11},{4,12},{5,7},{6,14},{7,5},{8,10},{9,1},{1... | collective-permute-start | bytes 835592 | tf_op jit(solution)/shard_map/cond/branch_0_fun/ppermute | solution.py:231
  54.9 18.5 %copy-start = (s32[16,16]{1,0:T(8,128)S(1)}, s32[16,16]{1,0:T(8,128)}, u32[]{:S(2)}) copy-start(s32[16,16]{1,0:T(8,128)} %refs_8_.1) | copy-start | bytes 3076
  54.9 18.5 %copy-start.1 = (s32[256]{0:T(256)S(1)}, s32[256]{0:T(256)}, u32[]{:S(2)}) copy-start(s32[256]{0:T(256)} %param.21) | copy-start | bytes 3076
  54.9 5.4 %collective-permute-start.22 = (f32[96,128]{1,0:T(8,128)S(1)}, f32[96,128]{1,0:T(8,128)S(1)}, u32[]{:S(2)}, u32[]{:S(2)}) collective-permute-start(f32[96,128]{1,0:T(8,128)S(1)} %get-tuple-element.98), channel_id=1, source_target_pairs={{0,4},{1,5},{2,6},{3,7},{4,8},{5,9},{6,10},{7,11},{8,12},{9,13},{1... | collective-permute-start | bytes 147464 | tf_op jit(solution)/shard_map/ppermute | solution.py:231
  55.4 5.9 %collective-permute-start.23 = (f32[96,128]{1,0:T(8,128)S(1)}, f32[96,128]{1,0:T(8,128)S(1)}, u32[]{:S(2)}, u32[]{:S(2)}) collective-permute-start(f32[96,128]{1,0:T(8,128)S(1)} %get-tuple-element.98), channel_id=1, source_target_pairs={{0,8},{1,9},{2,10},{3,11},{4,12},{5,13},{6,14},{7,15},{8,0},{9,1},... | collective-permute-start | bytes 147464 | tf_op jit(solution)/shard_map/ppermute | solution.py:231
  58.7 4.1 %collective-permute-start.24 = (f32[96,128]{1,0:T(8,128)S(1)}, f32[96,128]{1,0:T(8,128)S(1)}, u32[]{:S(2)}, u32[]{:S(2)}) collective-permute-start(f32[96,128]{1,0:T(8,128)S(1)} %get-tuple-element.98), channel_id=1, source_target_pairs={{0,12},{1,13},{2,14},{3,15},{4,0},{5,1},{6,2},{7,3},{8,4},{9,5},{1... | collective-permute-start | bytes 147464 | tf_op jit(solution)/shard_map/ppermute | solution.py:231
  62.8 8.5 %collective-permute-start.25 = (f32[384,128]{1,0:T(8,128)S(1)}, f32[384,128]{1,0:T(8,128)S(1)}, u32[]{:S(2)}, u32[]{:S(2)}) collective-permute-start(f32[384,128]{1,0:T(8,128)S(1)} %constant_dynamic-update-slice_fusion.refs_0_), channel_id=1, source_target_pairs={{0,1},{1,2},{2,3},{3,0},{4,5},{5,6},{6,7},{7,4},{8,9},{9,10},{10,1... | collective-permute-start | bytes 589832 | tf_op jit(solution)/shard_map/ppermute | solution.py:231
  62.9 10.5 %collective-permute-start.26 = (f32[384,128]{1,0:T(8,128)S(1)}, f32[384,128]{1,0:T(8,128)S(1)}, u32[]{:S(2)}, u32[]{:S(2)}) collective-permute-start(f32[384,128]{1,0:T(8,128)S(1)} %constant_dynamic-update-slice_fusion.refs_0_), channel_id=1, source_target_pairs={{0,2},{1,3},{2,0},{3,1},{4,6},{5,7},{6,4},{7,5},{8,10},{9,11},{10,... | collective-permute-start | bytes 589832 | tf_op jit(solution)/shard_map/ppermute | solution.py:231
  66.7 6.6 %collective-permute-start.27 = (f32[384,128]{1,0:T(8,128)S(1)}, f32[384,128]{1,0:T(8,128)S(1)}, u32[]{:S(2)}, u32[]{:S(2)}) collective-permute-start(f32[384,128]{1,0:T(8,128)S(1)} %constant_dynamic-update-slice_fusion.refs_0_), channel_id=1, source_target_pairs={{0,3},{1,0},{2,1},{3,2},{4,7},{5,4},{6,5},{7,6},{8,11},{9,8},{10,9... | collective-permute-start | bytes 589832 | tf_op jit(solution)/shard_map/ppermute | solution.py:231
  75.5 1.3 %collective-permute-start.28 = (f32[8,256]{1,0:T(8,128)S(1)}, f32[8,256]{1,0:T(8,128)S(1)}, u32[]{:S(2)}, u32[]{:S(2)}) collective-permute-start(f32[8,256]{1,0:T(8,128)S(1)} %get-tuple-element.75), channel_id=1, source_target_pairs={{0,16},{16,0},{32,48},{48,32},{64,80},{80,64},{96,112},{112,96},{1... | collective-permute-start | bytes 24584 | tf_op jit(solution)/shard_map/ppermute | solution.py:365
  76.8 4.0 %collective-permute-start.29 = (f32[8,256]{1,0:T(8,128)S(1)}, f32[8,256]{1,0:T(8,128)S(1)}, u32[]{:S(2)}, u32[]{:S(2)}) collective-permute-start(f32[8,256]{1,0:T(8,128)S(1)} %add.116), channel_id=1, source_target_pairs={{0,32},{16,48},{32,0},{48,16},{64,96},{80,112},{96,64},{112,80},{1... | collective-permute-start | bytes 24584 | tf_op jit(solution)/shard_map/ppermute | solution.py:365
  80.8 4.9 %collective-permute-start.30 = (f32[8,256]{1,0:T(8,128)S(1)}, f32[8,256]{1,0:T(8,128)S(1)}, u32[]{:S(2)}, u32[]{:S(2)}) collective-permute-start(f32[8,256]{1,0:T(8,128)S(1)} %add.117), channel_id=1, source_target_pairs={{0,96},{16,112},{32,64},{48,80},{64,32},{80,48},{96,0},{112,16},{1... | collective-permute-start | bytes 24584 | tf_op jit(solution)/shard_map/ppermute | solution.py:365
  (2 other events, 30.0 us)

commit v2 on v1

--- a/solution.py
+++ b/solution.py
@@ -91,13 +91,13 @@
     return (n + (m - 1)) // m * m
 
 
-def project_kernel(first, segs, cnts, acts, grads, w_in, w_out, *refs):
+def project_kernel(first, plans, acts, grads, w_in, w_out, *refs):
     outs, (act_buf, grad_buf, made_buf, spill, sems, out_sems) = refs[:4], refs[4:]
     toks = act_buf.shape[1]
     cap = outs[0].shape[0] // 2
 
     def copies(j):
-        s = segs[first + j]
+        s = plans[0, first + j]
         return (
             pltpu.make_async_copy(acts.at[s], act_buf.at[j], sems.at[j, 0]),
             pltpu.make_async_copy(grads.at[s], grad_buf.at[j], sems.at[j, 1]),
@@ -125,8 +125,8 @@
                     copy.wait()
             made = [rows(j + k) for k in range(SLOTS)]
             base = pl.multiple_of(i * cap, 8)
-            mid = pl.multiple_of(base + up(cnts[first + j], 8), 8)
-            last = pl.multiple_of(mid + up(cnts[first + j + 1], 8), 8)
+            mid = pl.multiple_of(base + up(plans[1, first + j], 8), 8)
+            last = pl.multiple_of(mid + up(plans[1, first + j + 1], 8), 8)
             out[pl.ds(base, toks), :] = made[0]
             out[pl.ds(mid, toks), :] = made[1]
             spill[...] = made[2]
@@ -136,16 +136,16 @@
                 out[pl.ds(to, 16), :] = spill[pl.ds(pl.multiple_of(n * 16, 16), 16), :]
                 return 0
 
-            return lax.fori_loop(0, up(cnts[first + j + 2], 16) // 16, piece, 0)
+            return lax.fori_loop(0, up(plans[1, first + j + 2], 16) // 16, piece, 0)
 
         lax.fori_loop(0, 2, block, 0)
-        leaving.append(pltpu.make_async_copy(out, outs[h], out_sems.at[h]))
+        leaving.append(pltpu.make_async_copy(out.at[pl.ds(0, 2 * cap)], outs[h], out_sems.at[h]))
         leaving[-1].start()
     for copy in leaving:
         copy.wait()
 
 
-def project(part, cap, segs, cnts, acts, grads_t, w_in, w_out):
+def project(part, cap, plans, acts, grads_t, w_in, w_out):
     toks, fa = acts.shape[1:]
     fg = grads_t.shape[1]
     n = acts.shape[0] // 2
@@ -154,13 +154,13 @@
     any_ = pl.BlockSpec(memory_space=pl.ANY)
     return pl.pallas_call(
         functools.partial(project_kernel, part * n),
-        in_specs=[smem, smem, any_, any_, vmem, vmem],
+        in_specs=[smem, any_, any_, vmem, vmem],
         out_specs=[any_] * 4,
         out_shape=[jax.ShapeDtypeStruct((2 * cap, 128), F32)] * 4,
         scratch_shapes=[
             pltpu.VMEM((n, toks, fa), BF16),
             pltpu.VMEM((n, fg, toks), BF16),
-            pltpu.VMEM((4, 2 * cap, 128), F32),
+            pltpu.VMEM((4, 2 * cap + 8, 128), F32),
             pltpu.VMEM((toks, 128), F32),
             pltpu.SemaphoreType.DMA((n, 2)),
             pltpu.SemaphoreType.DMA((4,)),
@@ -172,7 +172,7 @@
             transcendentals=0,
         ),
         name="project",
-    )(segs, cnts, acts, grads_t, w_in, w_out)
+    )(plans, acts, grads_t, w_in, w_out)
 
 
 def split(x):
@@ -180,7 +180,8 @@
     return hi, (x - hi.astype(F32)).astype(BF16)
 
 
-def outer_kernel(cnts, own, r1, r2, r3, out, pair):
+def outer_kernel(at, plans, own, r1, r2, r3, out, pair):
+    cnts = [plans[1, at + k] for k in range(SLOTS)]
     total = (own[...] + r1[...]) + (r2[...] + r3[...])
     cap = total.shape[0]
     row = lax.broadcasted_iota(jnp.int32, (cap, 128), 0)
@@ -212,11 +213,11 @@
     out[...] = jnp.where(lane < 64, first, other)
 
 
-def outer(cnts, parts):
+def outer(at, plans, parts):
     cap = parts[0].shape[0]
     spec = pl.BlockSpec(memory_space=pltpu.VMEM)
     return pl.pallas_call(
-        outer_kernel,
+        functools.partial(outer_kernel, at),
         in_specs=[pl.BlockSpec(memory_space=pltpu.SMEM)] + [spec] * 4,
         out_specs=spec,
         out_shape=jax.ShapeDtypeStruct((SLOTS * 32, 128), F32),
@@ -224,15 +225,15 @@
         compiler_params=pltpu.CompilerParams(vmem_limit_bytes=24 * 2**20),
         cost_estimate=pl.CostEstimate(flops=6 * 192 * cap * 128, bytes_accessed=4 * cap * 512, transcendentals=0),
         name="outer",
-    )(cnts, *parts)
+    )(plans, *parts)
 
 
 def hop(x, pairs):
     return lax.ppermute(x, "rank", pairs)
 
 
-def features(cap, segs, cnts, acts, grads_t, w_in, w_out):
-    made = [project(part, cap, segs, cnts, acts, grads_t, w_in, w_out) for part in range(2)]
+def features(cap, plans, acts, grads_t, w_in, w_out):
+    made = [project(part, cap, plans, acts, grads_t, w_in, w_out) for part in range(2)]
     made = [made[0][:2], made[0][2:], made[1][:2], made[1][2:]]
     flip = {1: 1, 2: 3}
     orders = [(stream, home) for stream in (1, 2) for home in (True, False)]
@@ -256,7 +257,7 @@
         hop(done[False, 2], SECOND[2]),
         hop(done[True, 2], SECOND[3]),
     ]
-    return outer(cnts[-4 * SLOTS :][:SLOTS], parts)
+    return outer(BLOCKS.index((True, 1, 0)) * SLOTS, plans, parts)
 
 
 def halves_kernel(queries, hi, lo):
@@ -280,7 +281,7 @@
     )(queries)
 
 
-def score_kernel(segs, *refs):
+def score_kernel(plans, *refs):
     feats, (q_hi, q_lo, seg_kind, query_kind, compat, raw_out, sums_out, placed) = refs[:4], refs[4:]
     n = placed.shape[0]
     nt = (((1,), (1,)), ((), ()))
@@ -301,7 +302,7 @@
         total = total + ((both[:n] + both[n:]) + dot(l_hi, q_lo[:, cols]))
     placed[...] = total
     for slot in range(n):
-        raw_out[pl.ds(segs[slot], 1), :] = placed[slot : slot + 1, :]
+        raw_out[pl.ds(plans[2, slot], 1), :] = placed[slot : slot + 1, :]
     kinds = compat.shape[0]
     one_seg = (seg_kind[...] == lax.broadcasted_iota(jnp.int32, (n, kinds), 1)).astype(F32)
     nq = query_kind.shape[1]
@@ -313,8 +314,8 @@
     sums_out[...] = jnp.broadcast_to(jnp.sum(raw * raw, axis=0, keepdims=True), sums_out.shape)
 
 
-def score(segs, feats, q_hi, q_lo, seg_emb, query_emb, compat):
-    n, (nq, nf) = segs.shape[0], q_hi.shape
+def score(plans, feats, q_hi, q_lo, seg_emb, query_emb, compat):
+    n, (nq, nf) = seg_emb.shape[0], q_hi.shape
     vmem = pl.BlockSpec(memory_space=pltpu.VMEM)
     return pl.pallas_call(
         score_kernel,
@@ -325,7 +326,48 @@
         compiler_params=pltpu.CompilerParams(vmem_limit_bytes=24 * 2**20),
         cost_estimate=pl.CostEstimate(flops=6 * n * nq * nf, bytes_accessed=nq * nf * 4, transcendentals=0),
         name="score",
-    )(segs, *feats, q_hi, q_lo, seg_emb[:, None], query_emb[None, :], compat)
+    )(plans, *feats, q_hi, q_lo, seg_emb[:, None], query_emb[None, :], compat)
+
+
+def plan_kernel(me, counts, positions, out):
+    n = counts.shape[1]
+    wide = 128
+    row = jnp.concatenate([counts[...], jnp.full((1, wide - n), -1, jnp.int32)], axis=1)
+    c_row = jnp.broadcast_to(row, (wide, wide)).astype(F32)
+    c_col = c_row.T
+    id_row = lax.broadcasted_iota(jnp.int32, (wide, wide), 1)
+    id_col = lax.broadcasted_iota(jnp.int32, (wide, wide), 0)
+    before = (c_row > c_col) | ((c_row == c_col) & (id_row < id_col))
+    place = jnp.sum(before.astype(jnp.int32), axis=1, keepdims=True)
+
+    def pick(where, values):
+        return jnp.sum(jnp.where(place == where, values, 0), axis=0, keepdims=True)
+
+    counts_col = c_col.astype(jnp.int32)
+    mine = positions[pl.ds(me[0], 1), :]
+    segs, cnts = pick(mine, id_col), pick(mine, counts_col)
+    back = pick(positions[pl.ds(me[0] + RANKS, 1), :], id_col)
+    held = [pick(positions[pl.ds(2 * RANKS + k, 1), :], counts_col) for k in range(SLOTS)]
+    load = sum(up(h, 8) for h in held)
+    need = jnp.broadcast_to(jnp.max(load, axis=1, keepdims=True), (1, wide))
+    rung = sum((need > cap).astype(jnp.int32) for cap in LADDER[:-1])
+    out[...] = jnp.concatenate([segs, cnts, back, rung] + [rung] * 4, axis=0)
+
+
+def plan(me, counts):
+    n = counts.shape[0]
+    table = np.full((40, 128), 127, np.int32)
+    table[:RANKS, :n] = PROJECT_POS
+    table[RANKS : 2 * RANKS, :n] = GATHER_POS
+    table[2 * RANKS : 2 * RANKS + SLOTS, :RANKS] = OWNER_POS.reshape(SLOTS, RANKS)
+    vmem = pl.BlockSpec(memory_space=pltpu.VMEM)
+    return pl.pallas_call(
+        plan_kernel,
+        in_specs=[pl.BlockSpec(memory_space=pltpu.SMEM), vmem, vmem],
+        out_specs=vmem,
+        out_shape=jax.ShapeDtypeStruct((8, 128), jnp.int32),
+        name="plan",
+    )(me[None], counts[None, :], jnp.asarray(table))
 
 
 def per_device(acts, grads, proj_in, proj_out, queries, seg_emb, query_emb, compat, counts):
@@ -334,30 +376,16 @@
     grads_t = jnp.swapaxes(grads, 1, 2)
     w_in, w_out = proj_in.T, proj_out.T
 
-    ids = lax.iota(jnp.int32, segs_here)
-    before = (counts[None, :] > counts[:, None]) | (
-        (counts[None, :] == counts[:, None]) & (ids[None, :] < ids[:, None])
-    )
-    place = jnp.sum(before.astype(jnp.int32), axis=1)
-
-    def pick(positions, values):
-        return jnp.sum(jnp.where(positions[:, None] == place[None, :], values[None, :], 0), axis=1)
-
-    mine = jnp.asarray(PROJECT_POS)[me]
-    segs, cnts = pick(mine, ids), pick(mine, counts)
-    segs_gathered = pick(jnp.asarray(GATHER_POS)[me], ids)
-
-    held = pick(jnp.asarray(OWNER_POS), counts).reshape(SLOTS, RANKS)
-    need = jnp.max(up(held[0], 8) + up(held[1], 8) + up(held[2], 16))
-    rung = jnp.sum((need > jnp.asarray(LADDER[:-1])).astype(jnp.int32))
+    plans = plan(me, counts)
+    rung = plans[3, 0]
     branches = [functools.partial(features, cap) for cap in LADDER]
-    owned = lax.switch(rung, branches, segs, cnts, acts, grads_t, w_in, w_out)
+    owned = lax.switch(rung, branches, plans, acts, grads_t, w_in, w_out)
     queries, owned = lax.optimization_barrier((queries, owned))
     q_hi, q_lo = halves(queries)
     line = jnp.concatenate([owned] + [hop(owned, shift(d, 0)) for d in (1, 2, 3)], axis=0)
     feats = [line] + [hop(line, shift(0, d)) for d in (1, 2, 3)]
     groups = lax.axis_size("dp")
-    raw, sums = score(segs_gathered, feats, q_hi, q_lo, seg_emb, query_emb, compat)
+    raw, sums = score(plans, feats, q_hi, q_lo, seg_emb, query_emb, compat)
 
     total = sums
     for core, z in ((1, 0), (0, 1), (0, 3)):

time: 86.9 us -> 85.7 us (0.986)
  other arithmetic: 3.45 us -> 0.92 us
  waiting for transfers between devices: 23.9 us -> 25.8 us
  Pallas kernels: 23.5 us -> 25.3 us
  starting transfers between devices: 33.4 us -> 31.8 us
    reduce_sum x2 -> x0, other arithmetic: 1.81 us -> none  [the longest x1 0.91 us: per_device(): place = jnp.sum(before.astype(jnp.int32), axis=1)]
    ppermute x17, waiting for transfers between devices: 19.3 us -> 20.6 us  [hop(): return lax.ppermute(x, 'rank', pairs)]
    pallas_call x1 -> x2, Pallas kernels: 1.15 us -> 2.34 us  [the longest x1 1.2 us: outer(): pl.pallas_call(functools.partial(outer_kernel, at), in_specs=[pl.BlockSpe...]
    ppermute x3, starting transfers between devices: 5.49 us -> 4.61 us  [per_device(): total = total + lax.ppermute(total, 'dp', other)]
  transfers between devices with their start and end apart: 20 -> 20, of which waited for: 13 -> 14; matrix products, arithmetic and copies ran while one was open for 1% -> 0% of each run, Pallas kernels for 14% -> 14%
where the time goes in v2:
time: 85.7 us; the launch traced here: 85.6 us
  starting transfers between devices  31.8 us (37%)
  waiting for transfers between devices  25.8 us (30%)
  Pallas kernels  25.3 us (30%)
  other arithmetic  0.92 us (1%)
    ppermute x17, starting transfers between devices, hop(): return lax.ppermute(x, 'rank', pairs)  27.2 us
    ppermute x17, waiting for transfers between devices, hop(): return lax.ppermute(x, 'rank', pairs)  20.6 us
    pallas_call x2, Pallas kernels, project(): pl.pallas_call(functools.partial(project_kernel, part * n), in_specs=[sme...  17.6 us
    ppermute x3, waiting for transfers between devices, per_device(): total = total + lax.ppermute(total, 'dp', other)  5.27 us
    ppermute x3, starting transfers between devices, per_device(): total = total + lax.ppermute(total, 'dp', other)  4.61 us
    pallas_call x1, Pallas kernels, halves(): pl.pallas_call(halves_kernel, grid=(steps,), in_specs=[spec], out_specs=[...  3.16 us
    pallas_call x1, Pallas kernels, score(): pl.pallas_call(score_kernel, in_specs=[pl.BlockSpec(memory_space=pltpu.SM...  2.21 us
  transfers between devices with their start and end apart: 20, of which 14 were waited for; matrix products, arithmetic and copies ran while one was open for 0% of the time, Pallas kernels for 14%

profile of v2, /device:TPU:0, one launch (start us, length us, event | category | flops | bytes accessed | tf_op | source)
XLA Modules:
  0.0 85.6 jit_solution(4510776857592520848)
XLA Ops:
  2.3 51.4 %conditional.1 = (f32[96,128]{1,0:T(8,128)S(1)}) conditional(s32[]{:T(128)} %bitcast.2, (s32[8,128]{1,0:T(8,128)S(1)}, bf16[48,256,256]{2,1,0:T(8,128)(2,1)}, bf16[48,688,256]{2,1,0:T(8,128)(2,1)}, bf16[64,256]{1,0:T(8,128)(2,1)}, bf16[64,688]{1,0:T(8,128)(2,1)}) %tuple.30, (s32[8,128]{1,0:T(8,128)S(1)}, bf16[48,256,256]{2,1,0:T(8,128)(2,1)}, ...), branch_computations={%region_0.0_spmd, %region_1.0_spmd} | conditional | flops 1599209472 | bytes 133784096 | solution.py:382
  2.4 8.5 %project.5 = (f32[1088,128]{1,0:T(8,128)S(1)}, f32[1088,128]{1,0:T(8,128)S(1)}, f32[1088,128]{1,0:T(8,128)S(1)}, f32[1088,128]{1,0:T(8,128)S(1)}) custom-call(s32[8,128]{1,0:T(8,128)S(1)} %get-tuple-element.28.plans, bf16[48,256,256]{2,1,0:T(8,128)(2,1)} %get-tuple-element.29.acts, bf16[48,688,256]{2,1,0:T(8,128)(2,1)} %get-tuple-element.30.grads, ...), custom_call_target="tpu_custom_call" | custom-call | flops 742391808 | bytes 13828096 | tf_op jit(solution)/shard_map/cond/branch_0_fun/project/pallas_call | solution.py:155
  12.2 3.3 %collective-permute-start.4 = (f32[1088,128]{1,0:T(8,128)S(1)}, f32[1088,128]{1,0:T(8,128)S(1)}, u32[]{:S(2)}, u32[]{:S(2)}) collective-permute-start(f32[1088,128]{1,0:T(8,128)S(1)} %get-tuple-element.38), channel_id=1, source_target_pairs={{0,3},{1,13},{2,1},{3,15},{4,8},{5,6},{6,10},{7,4},{8,11},{9,5},{1... | collective-permute-start | bytes 1671176 | tf_op jit(solution)/shard_map/cond/branch_0_fun/ppermute | solution.py:232
  15.5 1.9 %collective-permute-start.5 = (f32[1088,128]{1,0:T(8,128)S(1)}, f32[1088,128]{1,0:T(8,128)S(1)}, u32[]{:S(2)}, u32[]{:S(2)}) collective-permute-start(f32[1088,128]{1,0:T(8,128)S(1)} %get-tuple-element.39), channel_id=1, source_target_pairs={{0,12},{1,2},{2,14},{3,0},{4,7},{5,9},{6,5},{7,11},{8,4},{9,10},{1... | collective-permute-start | bytes 1671176 | tf_op jit(solution)/shard_map/cond/branch_0_fun/ppermute | solution.py:232
  17.4 9.1 %project.4 = (f32[1088,128]{1,0:T(8,128)S(1)}, f32[1088,128]{1,0:T(8,128)S(1)}, f32[1088,128]{1,0:T(8,128)S(1)}, f32[1088,128]{1,0:T(8,128)S(1)}) custom-call(s32[8,128]{1,0:T(8,128)S(1)} %get-tuple-element.28.plans, bf16[48,256,256]{2,1,0:T(8,128)(2,1)} %get-tuple-element.29.acts, bf16[48,688,256]{2,1,0:T(8,128)(2,1)S(1)} %copy-done.2, ...), custom_call_target="tpu_custom_call" | custom-call | flops 742391808 | bytes 13828096 | tf_op jit(solution)/shard_map/cond/branch_0_fun/project/pallas_call | solution.py:155
  27.5 2.2 %collective-permute-start.3 = (f32[544,128]{1,0:T(8,128)S(1)}, f32[544,128]{1,0:T(8,128)S(1)}, u32[]{:S(2)}, u32[]{:S(2)}) collective-permute-start(f32[544,128]{1,0:T(8,128)S(1)} %get-tuple-element.77), channel_id=1, source_target_pairs={{0,12},{1,2},{2,14},{3,0},{4,7},{5,9},{6,5},{7,11},{8,4},{9,10},{1... | collective-permute-start | bytes 835592 | tf_op jit(solution)/shard_map/cond/branch_0_fun/ppermute | solution.py:232
  30.2 2.1 %collective-permute-start.2 = (f32[544,128]{1,0:T(8,128)S(1)}, f32[544,128]{1,0:T(8,128)S(1)}, u32[]{:S(2)}, u32[]{:S(2)}) collective-permute-start(f32[544,128]{1,0:T(8,128)S(1)} %get-tuple-element.75), channel_id=1, source_target_pairs={{0,3},{1,13},{2,1},{3,15},{4,8},{5,6},{6,10},{7,4},{8,11},{9,5},{1... | collective-permute-start | bytes 835592 | tf_op jit(solution)/shard_map/cond/branch_0_fun/ppermute | solution.py:232
  33.0 1.4 %collective-permute-start.9 = (f32[544,128]{1,0:T(8,128)S(1)}, f32[544,128]{1,0:T(8,128)S(1)}, u32[]{:S(2)}, u32[]{:S(2)}) collective-permute-start(f32[544,128]{1,0:T(8,128)S(1)} %get-tuple-element.74), channel_id=1, source_target_pairs={{0,1},{1,5},{2,3},{3,7},{4,0},{5,4},{6,2},{7,6},{8,9},{9,13},{10,1... | collective-permute-start | bytes 835592 | tf_op jit(solution)/shard_map/cond/branch_0_fun/ppermute | solution.py:232
  34.4 1.6 %collective-permute-done.3 = f32[544,128]{1,0:T(8,128)S(1)} collective-permute-done((f32[544,128]{1,0:T(8,128)S(1)}, f32[544,128]{1,0:T(8,128)S(1)}, u32[]{:S(2)}, u32[]{:S(2)}) %collective-permute-start.3) | collective-permute-done | bytes 278560 | tf_op jit(solution)/shard_map/cond/branch_0_fun/ppermute | solution.py:232
  36.1 2.1 %collective-permute-done.2 = f32[544,128]{1,0:T(8,128)S(1)} collective-permute-done((f32[544,128]{1,0:T(8,128)S(1)}, f32[544,128]{1,0:T(8,128)S(1)}, u32[]{:S(2)}, u32[]{:S(2)}) %collective-permute-start.2) | collective-permute-done | bytes 278560 | tf_op jit(solution)/shard_map/cond/branch_0_fun/ppermute | solution.py:232
  39.9 1.5 %collective-permute-start.8 = (f32[544,128]{1,0:T(8,128)S(1)}, f32[544,128]{1,0:T(8,128)S(1)}, u32[]{:S(2)}, u32[]{:S(2)}) collective-permute-start(f32[544,128]{1,0:T(8,128)S(1)} %get-tuple-element.72), channel_id=1, source_target_pairs={{0,12},{1,0},{2,14},{3,2},{4,7},{5,1},{6,5},{7,3},{8,4},{9,8},{10,... | collective-permute-start | bytes 835592 | tf_op jit(solution)/shard_map/cond/branch_0_fun/ppermute | solution.py:232
  41.5 3.1 %collective-permute-start.10 = (f32[544,128]{1,0:T(8,128)S(1)}, f32[544,128]{1,0:T(8,128)S(1)}, u32[]{:S(2)}, u32[]{:S(2)}) collective-permute-start(f32[544,128]{1,0:T(8,128)S(1)} %get-tuple-element.70), channel_id=1, source_target_pairs={{0,2},{1,9},{2,0},{3,11},{4,12},{5,7},{6,14},{7,5},{8,10},{9,1},{1... | collective-permute-start | bytes 835592 | tf_op jit(solution)/shard_map/cond/branch_0_fun/ppermute | solution.py:232
  44.6 7.7 %collective-permute-done.6.r1 = f32[544,128]{1,0:T(8,128)S(1)} collective-permute-done((f32[544,128]{1,0:T(8,128)S(1)}, f32[544,128]{1,0:T(8,128)S(1)}, u32[]{:S(2)}, u32[]{:S(2)}) %collective-permute-start.6) | collective-permute-done | bytes 278560 | tf_op jit(solution)/shard_map/cond/branch_0_fun/ppermute | solution.py:232
  54.3 3.4 %collective-permute-start.23 = (f32[96,128]{1,0:T(8,128)S(1)}, f32[96,128]{1,0:T(8,128)S(1)}, u32[]{:S(2)}, u32[]{:S(2)}) collective-permute-start(f32[96,128]{1,0:T(8,128)S(1)} %get-tuple-element.86), channel_id=1, source_target_pairs={{0,8},{1,9},{2,10},{3,11},{4,12},{5,13},{6,14},{7,15},{8,0},{9,1},... | collective-permute-start | bytes 147464 | tf_op jit(solution)/shard_map/ppermute | solution.py:232
  57.7 1.5 %collective-permute-done.22 = f32[96,128]{1,0:T(8,128)S(1)} collective-permute-done((f32[96,128]{1,0:T(8,128)S(1)}, f32[96,128]{1,0:T(8,128)S(1)}, u32[]{:S(2)}, u32[]{:S(2)}) %collective-permute-start.22) | collective-permute-done | bytes 49184 | tf_op jit(solution)/shard_map/ppermute | solution.py:232
  60.2 1.5 %collective-permute-done.24 = f32[96,128]{1,0:T(8,128)S(1)} collective-permute-done((f32[96,128]{1,0:T(8,128)S(1)}, f32[96,128]{1,0:T(8,128)S(1)}, u32[]{:S(2)}, u32[]{:S(2)}) %collective-permute-start.24) | collective-permute-done | bytes 49184 | tf_op jit(solution)/shard_map/ppermute | solution.py:232
  61.7 3.9 %collective-permute-start.26 = (f32[384,128]{1,0:T(8,128)S(1)}, f32[384,128]{1,0:T(8,128)S(1)}, u32[]{:S(2)}, u32[]{:S(2)}) collective-permute-start(f32[384,128]{1,0:T(8,128)S(1)} %constant_dynamic-update-slice_fusion.refs_0_), channel_id=1, source_target_pairs={{0,2},{1,3},{2,0},{3,1},{4,6},{5,7},{6,4},{7,5},{8,10},{9,11},{10,... | collective-permute-start | bytes 589832 | tf_op jit(solution)/shard_map/ppermute | solution.py:232
  65.6 1.3 %collective-permute-start.27 = (f32[384,128]{1,0:T(8,128)S(1)}, f32[384,128]{1,0:T(8,128)S(1)}, u32[]{:S(2)}, u32[]{:S(2)}) collective-permute-start(f32[384,128]{1,0:T(8,128)S(1)} %constant_dynamic-update-slice_fusion.refs_0_), channel_id=1, source_target_pairs={{0,3},{1,0},{2,1},{3,2},{4,7},{5,4},{6,5},{7,6},{8,11},{9,8},{10,9... | collective-permute-start | bytes 589832 | tf_op jit(solution)/shard_map/ppermute | solution.py:232
  67.0 3.2 %halves.1 = (bf16[256,4096]{1,0:T(8,128)(2,1)S(1)}, bf16[256,4096]{1,0:T(8,128)(2,1)S(1)}) custom-call(f32[256,4096]{1,0:T(8,128)} %queries), custom_call_target="tpu_custom_call" | custom-call | flops 2097152 | bytes 8388608 | tf_op jit(solution)/shard_map/halves/pallas_call | solution.py:272
  70.7 2.2 %collective-permute-done.26.refs_2_ = f32[384,128]{1,0:T(8,128)S(1)} collective-permute-done((f32[384,128]{1,0:T(8,128)S(1)}, f32[384,128]{1,0:T(8,128)S(1)}, u32[]{:S(2)}, u32[]{:S(2)}) %collective-permute-start.26) | collective-permute-done | bytes 196640 | tf_op jit(solution)/shard_map/ppermute | solution.py:232
  72.9 2.2 %score.1 = (f32[48,256]{1,0:T(8,128)S(1)}, f32[8,256]{1,0:T(8,128)S(1)}) custom-call(s32[8,128]{1,0:T(8,128)S(1)} %plan.1.plans, f32[384,128]{1,0:T(8,128)S(1)} %constant_dynamic-update-slice_fusion.refs_0_, f32[384,128]{1,0:T(8,128)S(1)} %collective-permute-done.25.refs_1_, f32[384,128]{1,0:T(8,128)S(1)} %collective-permute-done.26.refs_2_, ...), custom_call_target="tpu_custom_call" | custom-call | flops 301989888 | bytes 4194304 | tf_op jit(solution)/shard_map/score/pallas_call | solution.py:320
  77.5 2.5 %collective-permute-done.29 = f32[8,256]{1,0:T(8,128)S(1)} collective-permute-done((f32[8,256]{1,0:T(8,128)S(1)}, f32[8,256]{1,0:T(8,128)S(1)}, u32[]{:S(2)}, u32[]{:S(2)}) %collective-permute-start.29) | collective-permute-done | bytes 8224 | tf_op jit(solution)/shard_map/ppermute | solution.py:393
  80.0 3.4 %collective-permute-start.30 = (f32[8,256]{1,0:T(8,128)S(1)}, f32[8,256]{1,0:T(8,128)S(1)}, u32[]{:S(2)}, u32[]{:S(2)}) collective-permute-start(f32[8,256]{1,0:T(8,128)S(1)} %add.88), channel_id=1, source_target_pairs={{0,96},{16,112},{32,64},{48,80},{64,32},{80,48},{96,0},{112,16},{1... | collective-permute-start | bytes 24584 | tf_op jit(solution)/shard_map/ppermute | solution.py:393
  83.4 1.6 %collective-permute-done.30 = f32[8,256]{1,0:T(8,128)S(1)} collective-permute-done((f32[8,256]{1,0:T(8,128)S(1)}, f32[8,256]{1,0:T(8,128)S(1)}, u32[]{:S(2)}, u32[]{:S(2)}) %collective-permute-start.30) | collective-permute-done | bytes 8224 | tf_op jit(solution)/shard_map/ppermute | solution.py:393
  (49 shorter events, 13.6 us)
Async XLA Ops:
  2.3 64.6 %copy-start.8 = (s32[48]{0:T(128)S(1)}, s32[48]{0:T(128)}, u32[]{:S(2)}) copy-start(s32[48]{0:T(128)} %param.17) | copy-start | bytes 580
  2.3 15.0 %copy-start.2 = (bf16[48,688,256]{2,1,0:T(8,128)(2,1)S(1)}, bf16[48,688,256]{2,1,0:T(8,128)(2,1)}, u32[]{:S(2)}) copy-start(bf16[48,688,256]{2,1,0:T(8,128)(2,1)} %get-tuple-element.30.grads) | copy-start | bytes 50724868 | tf_op jit(solution)/shard_map/cond
  10.9 15.6 %collective-permute-start = (f32[1088,128]{1,0:T(8,128)S(1)}, f32[1088,128]{1,0:T(8,128)S(1)}, u32[]{:S(2)}, u32[]{:S(2)}) collective-permute-start(f32[1088,128]{1,0:T(8,128)S(1)} %get-tuple-element.34), channel_id=1, source_target_pairs={{0,1},{1,5},{2,3},{3,7},{4,0},{5,4},{6,2},{7,6},{8,9},{9,13},{10,1... | collective-permute-start | bytes 1671176 | tf_op jit(solution)/shard_map/cond/branch_0_fun/ppermute | solution.py:232
  12.2 15.2 %collective-permute-start.4 = (f32[1088,128]{1,0:T(8,128)S(1)}, f32[1088,128]{1,0:T(8,128)S(1)}, u32[]{:S(2)}, u32[]{:S(2)}) collective-permute-start(f32[1088,128]{1,0:T(8,128)S(1)} %get-tuple-element.38), channel_id=1, source_target_pairs={{0,3},{1,13},{2,1},{3,15},{4,8},{5,6},{6,10},{7,4},{8,11},{9,5},{1... | collective-permute-start | bytes 1671176 | tf_op jit(solution)/shard_map/cond/branch_0_fun/ppermute | solution.py:232
  15.5 14.2 %collective-permute-start.1 = (f32[1088,128]{1,0:T(8,128)S(1)}, f32[1088,128]{1,0:T(8,128)S(1)}, u32[]{:S(2)}, u32[]{:S(2)}) collective-permute-start(f32[1088,128]{1,0:T(8,128)S(1)} %get-tuple-element.36), channel_id=1, source_target_pairs={{0,4},{1,0},{2,6},{3,2},{4,5},{5,1},{6,7},{7,3},{8,12},{9,8},{10,1... | collective-permute-start | bytes 1671176 | tf_op jit(solution)/shard_map/cond/branch_0_fun/ppermute | solution.py:232
  15.5 14.7 %collective-permute-start.5 = (f32[1088,128]{1,0:T(8,128)S(1)}, f32[1088,128]{1,0:T(8,128)S(1)}, u32[]{:S(2)}, u32[]{:S(2)}) collective-permute-start(f32[1088,128]{1,0:T(8,128)S(1)} %get-tuple-element.39), channel_id=1, source_target_pairs={{0,12},{1,2},{2,14},{3,0},{4,7},{5,9},{6,5},{7,11},{8,4},{9,10},{1... | collective-permute-start | bytes 1671176 | tf_op jit(solution)/shard_map/cond/branch_0_fun/ppermute | solution.py:232
  27.5 8.6 %collective-permute-start.3 = (f32[544,128]{1,0:T(8,128)S(1)}, f32[544,128]{1,0:T(8,128)S(1)}, u32[]{:S(2)}, u32[]{:S(2)}) collective-permute-start(f32[544,128]{1,0:T(8,128)S(1)} %get-tuple-element.77), channel_id=1, source_target_pairs={{0,12},{1,2},{2,14},{3,0},{4,7},{5,9},{6,5},{7,11},{8,4},{9,10},{1... | collective-permute-start | bytes 835592 | tf_op jit(solution)/shard_map/cond/branch_0_fun/ppermute | solution.py:232
  30.2 7.9 %collective-permute-start.2 = (f32[544,128]{1,0:T(8,128)S(1)}, f32[544,128]{1,0:T(8,128)S(1)}, u32[]{:S(2)}, u32[]{:S(2)}) collective-permute-start(f32[544,128]{1,0:T(8,128)S(1)} %get-tuple-element.75), channel_id=1, source_target_pairs={{0,3},{1,13},{2,1},{3,15},{4,8},{5,6},{6,10},{7,4},{8,11},{9,5},{1... | collective-permute-start | bytes 835592 | tf_op jit(solution)/shard_map/cond/branch_0_fun/ppermute | solution.py:232
  32.4 6.7 %collective-permute-start.7 = (f32[544,128]{1,0:T(8,128)S(1)}, f32[544,128]{1,0:T(8,128)S(1)}, u32[]{:S(2)}, u32[]{:S(2)}) collective-permute-start(f32[544,128]{1,0:T(8,128)S(1)} %get-tuple-element.76), channel_id=1, source_target_pairs={{0,4},{1,0},{2,6},{3,2},{4,5},{5,1},{6,7},{7,3},{8,12},{9,8},{10,1... | collective-permute-start | bytes 835592 | tf_op jit(solution)/shard_map/cond/branch_0_fun/ppermute | solution.py:232
  33.0 8.4 %collective-permute-start.9 = (f32[544,128]{1,0:T(8,128)S(1)}, f32[544,128]{1,0:T(8,128)S(1)}, u32[]{:S(2)}, u32[]{:S(2)}) collective-permute-start(f32[544,128]{1,0:T(8,128)S(1)} %get-tuple-element.74), channel_id=1, source_target_pairs={{0,1},{1,5},{2,3},{3,7},{4,0},{5,4},{6,2},{7,6},{8,9},{9,13},{10,1... | collective-permute-start | bytes 835592 | tf_op jit(solution)/shard_map/cond/branch_0_fun/ppermute | solution.py:232
  39.2 13.1 %collective-permute-start.6 = (f32[544,128]{1,0:T(8,128)S(1)}, f32[544,128]{1,0:T(8,128)S(1)}, u32[]{:S(2)}, u32[]{:S(2)}) collective-permute-start(f32[544,128]{1,0:T(8,128)S(1)} %get-tuple-element.73), channel_id=1, source_target_pairs={{0,4},{1,2},{2,6},{3,0},{4,5},{5,9},{6,7},{7,11},{8,12},{9,10},{10... | collective-permute-start | bytes 835592 | tf_op jit(solution)/shard_map/cond/branch_0_fun/ppermute | solution.py:232
  39.9 12.4 %collective-permute-start.8 = (f32[544,128]{1,0:T(8,128)S(1)}, f32[544,128]{1,0:T(8,128)S(1)}, u32[]{:S(2)}, u32[]{:S(2)}) collective-permute-start(f32[544,128]{1,0:T(8,128)S(1)} %get-tuple-element.72), channel_id=1, source_target_pairs={{0,12},{1,0},{2,14},{3,2},{4,7},{5,1},{6,5},{7,3},{8,4},{9,8},{10,... | collective-permute-start | bytes 835592 | tf_op jit(solution)/shard_map/cond/branch_0_fun/ppermute | solution.py:232
  41.5 10.8 %collective-permute-start.10 = (f32[544,128]{1,0:T(8,128)S(1)}, f32[544,128]{1,0:T(8,128)S(1)}, u32[]{:S(2)}, u32[]{:S(2)}) collective-permute-start(f32[544,128]{1,0:T(8,128)S(1)} %get-tuple-element.70), channel_id=1, source_target_pairs={{0,2},{1,9},{2,0},{3,11},{4,12},{5,7},{6,14},{7,5},{8,10},{9,1},{1... | collective-permute-start | bytes 835592 | tf_op jit(solution)/shard_map/cond/branch_0_fun/ppermute | solution.py:232
  53.7 19.1 %copy-start = (s32[16,16]{1,0:T(8,128)S(1)}, s32[16,16]{1,0:T(8,128)}, u32[]{:S(2)}) copy-start(s32[16,16]{1,0:T(8,128)} %refs_8_.1) | copy-start | bytes 3076
  53.7 19.1 %copy-start.1 = (s32[256]{0:T(256)S(1)}, s32[256]{0:T(256)}, u32[]{:S(2)}) copy-start(s32[256]{0:T(256)} %param.18) | copy-start | bytes 3076
  53.8 5.4 %collective-permute-start.22 = (f32[96,128]{1,0:T(8,128)S(1)}, f32[96,128]{1,0:T(8,128)S(1)}, u32[]{:S(2)}, u32[]{:S(2)}) collective-permute-start(f32[96,128]{1,0:T(8,128)S(1)} %get-tuple-element.86), channel_id=1, source_target_pairs={{0,4},{1,5},{2,6},{3,7},{4,8},{5,9},{6,10},{7,11},{8,12},{9,13},{1... | collective-permute-start | bytes 147464 | tf_op jit(solution)/shard_map/ppermute | solution.py:232
  54.3 5.9 %collective-permute-start.23 = (f32[96,128]{1,0:T(8,128)S(1)}, f32[96,128]{1,0:T(8,128)S(1)}, u32[]{:S(2)}, u32[]{:S(2)}) collective-permute-start(f32[96,128]{1,0:T(8,128)S(1)} %get-tuple-element.86), channel_id=1, source_target_pairs={{0,8},{1,9},{2,10},{3,11},{4,12},{5,13},{6,14},{7,15},{8,0},{9,1},... | collective-permute-start | bytes 147464 | tf_op jit(solution)/shard_map/ppermute | solution.py:232
  57.6 4.1 %collective-permute-start.24 = (f32[96,128]{1,0:T(8,128)S(1)}, f32[96,128]{1,0:T(8,128)S(1)}, u32[]{:S(2)}, u32[]{:S(2)}) collective-permute-start(f32[96,128]{1,0:T(8,128)S(1)} %get-tuple-element.86), channel_id=1, source_target_pairs={{0,12},{1,13},{2,14},{3,15},{4,0},{5,1},{6,2},{7,3},{8,4},{9,5},{1... | collective-permute-start | bytes 147464 | tf_op jit(solution)/shard_map/ppermute | solution.py:232
  61.7 9.0 %collective-permute-start.25 = (f32[384,128]{1,0:T(8,128)S(1)}, f32[384,128]{1,0:T(8,128)S(1)}, u32[]{:S(2)}, u32[]{:S(2)}) collective-permute-start(f32[384,128]{1,0:T(8,128)S(1)} %constant_dynamic-update-slice_fusion.refs_0_), channel_id=1, source_target_pairs={{0,1},{1,2},{2,3},{3,0},{4,5},{5,6},{6,7},{7,4},{8,9},{9,10},{10,1... | collective-permute-start | bytes 589832 | tf_op jit(solution)/shard_map/ppermute | solution.py:232
  61.7 11.2 %collective-permute-start.26 = (f32[384,128]{1,0:T(8,128)S(1)}, f32[384,128]{1,0:T(8,128)S(1)}, u32[]{:S(2)}, u32[]{:S(2)}) collective-permute-start(f32[384,128]{1,0:T(8,128)S(1)} %constant_dynamic-update-slice_fusion.refs_0_), channel_id=1, source_target_pairs={{0,2},{1,3},{2,0},{3,1},{4,6},{5,7},{6,4},{7,5},{8,10},{9,11},{10,... | collective-permute-start | bytes 589832 | tf_op jit(solution)/shard_map/ppermute | solution.py:232
  65.6 7.3 %collective-permute-start.27 = (f32[384,128]{1,0:T(8,128)S(1)}, f32[384,128]{1,0:T(8,128)S(1)}, u32[]{:S(2)}, u32[]{:S(2)}) collective-permute-start(f32[384,128]{1,0:T(8,128)S(1)} %constant_dynamic-update-slice_fusion.refs_0_), channel_id=1, source_target_pairs={{0,3},{1,0},{2,1},{3,2},{4,7},{5,4},{6,5},{7,6},{8,11},{9,8},{10,9... | collective-permute-start | bytes 589832 | tf_op jit(solution)/shard_map/ppermute | solution.py:232
  75.1 1.3 %collective-permute-start.28 = (f32[8,256]{1,0:T(8,128)S(1)}, f32[8,256]{1,0:T(8,128)S(1)}, u32[]{:S(2)}, u32[]{:S(2)}) collective-permute-start(f32[8,256]{1,0:T(8,128)S(1)} %get-tuple-element.69), channel_id=1, source_target_pairs={{0,16},{16,0},{32,48},{48,32},{64,80},{80,64},{96,112},{112,96},{1... | collective-permute-start | bytes 24584 | tf_op jit(solution)/shard_map/ppermute | solution.py:393
  76.3 3.7 %collective-permute-start.29 = (f32[8,256]{1,0:T(8,128)S(1)}, f32[8,256]{1,0:T(8,128)S(1)}, u32[]{:S(2)}, u32[]{:S(2)}) collective-permute-start(f32[8,256]{1,0:T(8,128)S(1)} %add.87), channel_id=1, source_target_pairs={{0,32},{16,48},{32,0},{48,16},{64,96},{80,112},{96,64},{112,80},{1... | collective-permute-start | bytes 24584 | tf_op jit(solution)/shard_map/ppermute | solution.py:393
  80.0 5.0 %collective-permute-start.30 = (f32[8,256]{1,0:T(8,128)S(1)}, f32[8,256]{1,0:T(8,128)S(1)}, u32[]{:S(2)}, u32[]{:S(2)}) collective-permute-start(f32[8,256]{1,0:T(8,128)S(1)} %add.88), channel_id=1, source_target_pairs={{0,96},{16,112},{32,64},{48,80},{64,32},{80,48},{96,0},{112,16},{1... | collective-permute-start | bytes 24584 | tf_op jit(solution)/shard_map/ppermute | solution.py:393
  (2 other events, 30.0 us)
